TPU v7x, 32 devices: a whole 2x2x4 slice. The times are simulated.
32 devices in a mesh: path: 2 (over core), dp: 16 (over z, y, x).
Axes of the slice: x: 2, y: 2, z: 4, core: 2. Of those that a mesh axis runs over, the one named last changes fastest.
Arguments:
- slow_in: bfloat16 [2, 128, 196, 1024], P(None, ('path', 'dp')), may hold values from -6 to 6
- fast_in: bfloat16 [2, 512, 196, 128], P(None, ('path', 'dp')), may hold values from -6 to 6
- clip_starts: int32 [2, 128], P(None, ('path', 'dp')), may hold values from 0 to 1, as said below
- w_lateral: bfloat16 [163840], P(('path', 'dp')), may hold values from -0.25 to 0.25
- w_slow_time: bfloat16 [983040], P(('path', 'dp')), may hold values from -0.09375 to 0.09375
- w_slow_space: bfloat16 [589824], P(('path', 'dp')), may hold values from -0.125 to 0.125
- w_slow_out: bfloat16 [262144], P(('path', 'dp')), may hold values from -0.375 to 0.375
- w_projection: bfloat16 [1310720], P(('path', 'dp')), may hold values from -0.15625 to 0.15625
- w_fast_time: bfloat16 [12288], P(('path', 'dp')), may hold values from -0.3125 to 0.3125
- w_fast_space: bfloat16 [9216], P(('path', 'dp')), may hold values from -0.375 to 0.375
- w_fast_out: bfloat16 [4096], P(('path', 'dp')), may hold values from -1 to 1
- slow_gain: bfloat16 [2816], P(('path', 'dp')), may hold values from 0.25 to 1.75
- slow_bias: bfloat16 [2816], P(('path', 'dp')), may hold values from -3 to 3
- fast_gain: bfloat16 [192], replicated, may hold values from 0.25 to 1.75
- fast_bias: bfloat16 [192], replicated, may hold values from -3 to 3
- slow_cotangent: bfloat16 [2, 128, 196, 1024], P(None, ('path', 'dp')), may hold values from -6 to 6
- fast_cotangent: bfloat16 [2, 512, 196, 128], P(None, ('path', 'dp')), may hold values from -6 to 6
Outputs:
- slow_out: bfloat16 [2, 128, 196, 1024], P(None, ('path', 'dp'))
- fast_out: bfloat16 [2, 512, 196, 128], P(None, ('path', 'dp'))
- slow_in_grad: bfloat16 [2, 128, 196, 1024], P(None, ('path', 'dp'))
- fast_in_grad: bfloat16 [2, 512, 196, 128], P(None, ('path', 'dp'))
- lateral_grad: float32 [163840], P(('path', 'dp'))
- slow_time_grad: float32 [983040], P(('path', 'dp'))
- slow_space_grad: float32 [589824], P(('path', 'dp'))
- slow_out_grad: float32 [262144], P(('path', 'dp'))
- projection_grad: float32 [1310720], P(('path', 'dp'))
- fast_time_grad: float32 [12288], P(('path', 'dp'))
- fast_space_grad: float32 [9216], P(('path', 'dp'))
- fast_out_grad: float32 [4096], P(('path', 'dp'))
- slow_gain_grad: float32 [2816], P(('path', 'dp'))
- slow_bias_grad: float32 [2816], P(('path', 'dp'))
- fast_gain_grad: float32 [192], replicated
- fast_bias_grad: float32 [192], replicated
Inputs may be any that keep to these rules, and one draw needn't show every extreme that they name: `clip_starts`: 1 marks the first slow frame of a clip; frame 0 of every stream is 1; clips never span streams.
All inputs are finite; a program needn't handle non-finite values.
Results may differ from a plain program's by a relative error of at most 0.0085.
Values may be sent and summed in bfloat16 or wider, within the bound.
No kernel may reach another device: no remote copies, remote signals or barrier semaphores. Data moves between devices by JAX's collectives and lax.ppermute only.
A program may use at most 256 MiB of HBM per device.

v0:
```python
import jax
import jax.numpy as jnp
from jax import lax
from jax.sharding import PartitionSpec as P

CS = 1024
CL = 256
CM = 256
CF = 128
CFM = 32
HH = 14
WW = 14


EPS = 1e-05


def padded_2(cells, sides, width):
    for axis, dim in sides:
        count = lax.axis_size(axis)
        ends = count - 1
        head = lax.slice_in_dim(cells, 0, width, axis=dim)
        tail = lax.slice_in_dim(cells, cells.shape[dim] - width, cells.shape[dim], axis=dim)
        cells = jnp.concatenate(
            [
                lax.ppermute(tail, axis, [(i, (i + 1) % count) for i in range(ends)]),
                cells,
                lax.ppermute(head, axis, [((i + 1) % count, i) for i in range(ends)]),
            ],
            axis=dim,
        )
    return cells


def smooth(inputs):
    return jax.nn.gelu(inputs, approximate=True)


def smooth_back(inputs, grad_out):
    return jax.vjp(smooth, inputs)[1](grad_out)[0]


def matmul(inputs, weight):
    flat_in = inputs.reshape(-1, inputs.shape[-1])
    result = jnp.dot(flat_in, weight, preferred_element_type=jnp.float32)
    return result.reshape(inputs.shape[:-1] + (weight.shape[-1],))


def weight_term(inputs, grads):
    return lax.dot_general(
        inputs.reshape(-1, inputs.shape[-1]),
        grads.reshape(-1, grads.shape[-1]),
        (((0,), (0,)), ((), ())),
        preferred_element_type=jnp.float32,
    )


def space_taps(frames):
    grid_cells = frames.reshape(frames.shape[0], HH, WW, frames.shape[-1])
    padded = jnp.pad(grid_cells, ((0, 0), (1, 1), (1, 1), (0, 0)))
    return [
        padded[:, row_at : row_at + HH, col_at : col_at + WW, :].reshape(frames.shape)
        for row_at in range(3)
        for col_at in range(3)
    ]


def in_space(frames, weight):
    tap_list = space_taps(frames)
    result = matmul(tap_list[0], weight[0])
    for tap_num in range(1, 9):
        result = result + matmul(tap_list[tap_num], weight[tap_num])
    return result


def space_back(grads, weight):
    flipped = jnp.transpose(jnp.flip(weight, 0), (0, 2, 1))
    return in_space(grads, flipped)


def space_weight(frames, grads):
    return jnp.stack([weight_term(tap_item, grads) for tap_item in space_taps(frames)], 0)


def split_parts(vector, extents):
    parts_out = []
    start_at = 0
    for extent in extents:
        parts_out.append(vector[start_at : start_at + extent])
        start_at += extent
    return parts_out


def norm_totals(tensors):
    firsts = [jnp.sum(tensor, (0, 1)) for tensor in tensors]
    seconds = [jnp.sum(tensor * tensor, (0, 1)) for tensor in tensors]
    joined = lax.psum(jnp.concatenate(firsts + seconds), ("path", "dp"))
    extents = [tensor.shape[-1] for tensor in tensors]
    pieces = split_parts(joined, extents + extents)
    return (pieces[: len(tensors)], pieces[len(tensors) :])


def normalize(pre_norm, first_sum, second_sum, count, gain_vec, bias_vec):
    mean_val = first_sum / count
    scale_val = lax.rsqrt(second_sum / count - mean_val * mean_val + EPS)
    normed = (pre_norm - mean_val) * scale_val
    return (normed * gain_vec + bias_vec, normed, scale_val)


def grad_totals(vectors):
    joined = lax.psum(jnp.concatenate(vectors), ("path", "dp"))
    return split_parts(joined, [vector.shape[0] for vector in vectors])


def norm_back(grad_out, normed, scale_val, gain_vec, sum_one, sum_two, count):
    return gain_vec * scale_val * (grad_out - sum_one / count - normed * (sum_two / count))


def local_sums(grad_out, normed):
    return (jnp.sum(grad_out, (0, 1)), jnp.sum(grad_out * normed, (0, 1)))


def unpack(gathered):
    shapes = [
        (5, CF, CL),
        (3, CS + CL, CM),
        (9, CM, CM),
        (CM, CS),
        (CS + CL, CS),
        (3, CF, CFM),
        (9, CFM, CFM),
        (CFM, CF),
    ]
    weights = [gathered[place].reshape(shapes[place]) for place in range(8)]
    slow_gains = split_parts(gathered[8].astype(jnp.float32), [CL, CM, CM, CS, CS])
    slow_biases = split_parts(gathered[9].astype(jnp.float32), [CL, CM, CM, CS, CS])
    return (weights, slow_gains, slow_biases)


def local(
    slow_in,
    fast_in,
    clip_starts,
    w_lateral,
    w_slow_time,
    w_slow_space,
    w_slow_out,
    w_projection,
    w_fast_time,
    w_fast_space,
    w_fast_out,
    slow_gain,
    slow_bias,
    fast_gain,
    fast_bias,
    slow_cotangent,
    fast_cotangent,
):
    devices = lax.axis_size(("path", "dp"))
    fast_gains = split_parts(fast_gain.astype(jnp.float32), [CFM, CFM, CF])
    fast_biases = split_parts(fast_bias.astype(jnp.float32), [CFM, CFM, CF])
    weight_acc = [
        jnp.zeros(shape_of, jnp.float32)
        for shape_of in [
            (5, CF, CL),
            (3, CS + CL, CM),
            (9, CM, CM),
            (CM, CS),
            (CS + CL, CS),
            (3, CF, CFM),
            (9, CFM, CFM),
            (CFM, CF),
        ]
    ]
    slow_gain_acc = [jnp.zeros((extent,), jnp.float32) for extent in [CL, CM, CM, CS, CS]]
    slow_bias_acc = [jnp.zeros((extent,), jnp.float32) for extent in [CL, CM, CM, CS, CS]]
    fast_gain_acc = [jnp.zeros((extent,), jnp.float32) for extent in [CFM, CFM, CF]]
    fast_bias_acc = [jnp.zeros((extent,), jnp.float32) for extent in [CFM, CFM, CF]]
    slow_outs = []
    fast_outs = []
    slow_grads_out = []
    fast_grads_out = []
    for micro_step in range(slow_in.shape[0]):
        gathered = (
            lax.all_gather(w_lateral, ("path", "dp"), axis=0, tiled=True),
            lax.all_gather(w_slow_time, ("path", "dp"), axis=0, tiled=True),
            lax.all_gather(w_slow_space, ("path", "dp"), axis=0, tiled=True),
            lax.all_gather(w_slow_out, ("path", "dp"), axis=0, tiled=True),
            lax.all_gather(w_projection, ("path", "dp"), axis=0, tiled=True),
            lax.all_gather(w_fast_time, ("path", "dp"), axis=0, tiled=True),
            lax.all_gather(w_fast_space, ("path", "dp"), axis=0, tiled=True),
            lax.all_gather(w_fast_out, ("path", "dp"), axis=0, tiled=True),
            lax.all_gather(slow_gain, ("path", "dp"), axis=0, tiled=True),
            lax.all_gather(slow_bias, ("path", "dp"), axis=0, tiled=True),
        )
        weights, slow_gains, slow_biases = unpack(gathered)
        lateral, slow_time, slow_space, slow_proj, projection, fast_time, fast_space, fast_proj = (
            weights
        )
        slow_block = slow_in[micro_step]
        fast_block = fast_in[micro_step]
        frames = slow_block.shape[0]
        slow_link = 1 - clip_starts[micro_step]
        fast_link = jnp.where(lax.iota(jnp.int32, 4 * frames) % 4 == 0, jnp.repeat(slow_link, 4), 1)
        slow_mask = slow_link.astype(jnp.bfloat16)[:, None, None]
        fast_mask = fast_link.astype(jnp.bfloat16)[:, None, None]
        slow_count = float(frames * slow_block.shape[1] * devices)
        fast_count = 4.0 * slow_count
        fast_edges = jnp.stack(
            [
                fast_block[0] * fast_mask[0],
                jnp.zeros_like(fast_block[0]),
                fast_block[-2],
                fast_block[-1],
            ],
            0,
        )
        fast_rim = padded_2(fast_edges, ((("path", "dp"), 0),), 2)
        quads = fast_block.reshape(frames, 4, fast_block.shape[1], fast_block.shape[2])
        third = jnp.concatenate([fast_rim[0][None], quads[:-1, 2]], 0) * slow_mask
        fourth = jnp.concatenate([fast_rim[1][None], quads[:-1, 3]], 0) * slow_mask
        lat_pre = matmul(third, lateral[0]) + matmul(fourth, lateral[1])
        for tap_num in range(3):
            lat_pre = lat_pre + matmul(quads[:, tap_num], lateral[tap_num + 2])
        fast_before = jnp.concatenate([fast_rim[1][None], fast_block[:-1]], 0) * fast_mask
        fast_after = jnp.concatenate([fast_block[1:] * fast_mask[1:], fast_rim[6][None]], 0)
        fast_one = (
            matmul(fast_before, fast_time[0])
            + matmul(fast_block, fast_time[1])
            + matmul(fast_after, fast_time[2])
        )
        firsts, seconds = norm_totals([lat_pre, fast_one])
        lat_norm, lat_hat, lat_scale = normalize(
            lat_pre, firsts[0], seconds[0], slow_count, slow_gains[0], slow_biases[0]
        )
        fone_norm, fone_hat, fone_scale = normalize(
            fast_one, firsts[1], seconds[1], fast_count, fast_gains[0], fast_biases[0]
        )
        lat_act = smooth(lat_norm).astype(jnp.bfloat16)
        joined = jnp.concatenate([slow_block, lat_act], -1)
        slow_edges = jnp.stack([joined[0] * slow_mask[0], joined[-1]], 0)
        slow_rim = padded_2(slow_edges, ((("path", "dp"), 0),), 1)
        slow_before = jnp.concatenate([slow_rim[0][None], joined[:-1]], 0) * slow_mask
        slow_after = jnp.concatenate([joined[1:] * slow_mask[1:], slow_rim[3][None]], 0)
        slow_one = (
            matmul(slow_before, slow_time[0])
            + matmul(joined, slow_time[1])
            + matmul(slow_after, slow_time[2])
        )
        short_pre = matmul(joined, projection)
        fact_one = smooth(fone_norm).astype(jnp.bfloat16)
        fast_two = in_space(fact_one, fast_space)
        firsts, seconds = norm_totals([slow_one, short_pre, fast_two])
        sone_norm, sone_hat, sone_scale = normalize(
            slow_one, firsts[0], seconds[0], slow_count, slow_gains[1], slow_biases[1]
        )
        short_norm, short_hat, short_scale = normalize(
            short_pre, firsts[1], seconds[1], slow_count, slow_gains[4], slow_biases[4]
        )
        ftwo_norm, ftwo_hat, ftwo_scale = normalize(
            fast_two, firsts[2], seconds[2], fast_count, fast_gains[1], fast_biases[1]
        )
        act_one = smooth(sone_norm).astype(jnp.bfloat16)
        slow_two = in_space(act_one, slow_space)
        fact_two = smooth(ftwo_norm).astype(jnp.bfloat16)
        fast_three = matmul(fact_two, fast_proj)
        firsts, seconds = norm_totals([slow_two, fast_three])
        stwo_norm, stwo_hat, stwo_scale = normalize(
            slow_two, firsts[0], seconds[0], slow_count, slow_gains[2], slow_biases[2]
        )
        fthree_norm, fthree_hat, fthree_scale = normalize(
            fast_three, firsts[1], seconds[1], fast_count, fast_gains[2], fast_biases[2]
        )
        act_two = smooth(stwo_norm).astype(jnp.bfloat16)
        slow_three = matmul(act_two, slow_proj)
        fast_total = fthree_norm + fast_block.astype(jnp.float32)
        fast_outs.append(smooth(fast_total).astype(jnp.bfloat16))
        firsts, seconds = norm_totals([slow_three])
        sthree_norm, sthree_hat, sthree_scale = normalize(
            slow_three, firsts[0], seconds[0], slow_count, slow_gains[3], slow_biases[3]
        )
        slow_total = sthree_norm + short_norm
        slow_outs.append(smooth(slow_total).astype(jnp.bfloat16))
        regathered = (
            lax.all_gather(w_lateral, ("path", "dp"), axis=0, tiled=True),
            lax.all_gather(w_slow_time, ("path", "dp"), axis=0, tiled=True),
            lax.all_gather(w_slow_space, ("path", "dp"), axis=0, tiled=True),
            lax.all_gather(w_slow_out, ("path", "dp"), axis=0, tiled=True),
            lax.all_gather(w_projection, ("path", "dp"), axis=0, tiled=True),
            lax.all_gather(w_fast_time, ("path", "dp"), axis=0, tiled=True),
            lax.all_gather(w_fast_space, ("path", "dp"), axis=0, tiled=True),
            lax.all_gather(w_fast_out, ("path", "dp"), axis=0, tiled=True),
            lax.all_gather(slow_gain, ("path", "dp"), axis=0, tiled=True),
            lax.all_gather(slow_bias, ("path", "dp"), axis=0, tiled=True),
        )
        weights, slow_gains, slow_biases = unpack(regathered)
        lateral, slow_time, slow_space, slow_proj, projection, fast_time, fast_space, fast_proj = (
            weights
        )
        slow_grad = smooth_back(slow_total, slow_cotangent[micro_step].astype(jnp.float32))
        fast_grad = smooth_back(fast_total, fast_cotangent[micro_step].astype(jnp.float32))
        sums_a = local_sums(slow_grad, sthree_hat)
        sums_b = local_sums(slow_grad, short_hat)
        sums_c = local_sums(fast_grad, fthree_hat)
        totals = grad_totals([sums_a[0], sums_a[1], sums_b[0], sums_b[1], sums_c[0], sums_c[1]])
        slow_gain_acc[3] = slow_gain_acc[3] + totals[1]
        slow_bias_acc[3] = slow_bias_acc[3] + totals[0]
        slow_gain_acc[4] = slow_gain_acc[4] + totals[3]
        slow_bias_acc[4] = slow_bias_acc[4] + totals[2]
        fast_gain_acc[2] = fast_gain_acc[2] + totals[5]
        fast_bias_acc[2] = fast_bias_acc[2] + totals[4]
        d_three = norm_back(
            slow_grad, sthree_hat, sthree_scale, slow_gains[3], totals[0], totals[1], slow_count
        ).astype(jnp.bfloat16)
        d_short = norm_back(
            slow_grad, short_hat, short_scale, slow_gains[4], totals[2], totals[3], slow_count
        ).astype(jnp.bfloat16)
        d_fthree = norm_back(
            fast_grad, fthree_hat, fthree_scale, fast_gains[2], totals[4], totals[5], fast_count
        ).astype(jnp.bfloat16)
        weight_acc[3] = weight_acc[3] + weight_term(act_two, d_three)
        weight_acc[7] = weight_acc[7] + weight_term(fact_two, d_fthree)
        grad_two = smooth_back(stwo_norm, matmul(d_three, slow_proj.T))
        fgrad_two = smooth_back(ftwo_norm, matmul(d_fthree, fast_proj.T))
        sums_a = local_sums(grad_two, stwo_hat)
        sums_c = local_sums(fgrad_two, ftwo_hat)
        totals = grad_totals([sums_a[0], sums_a[1], sums_c[0], sums_c[1]])
        slow_gain_acc[2] = slow_gain_acc[2] + totals[1]
        slow_bias_acc[2] = slow_bias_acc[2] + totals[0]
        fast_gain_acc[1] = fast_gain_acc[1] + totals[3]
        fast_bias_acc[1] = fast_bias_acc[1] + totals[2]
        d_two = norm_back(
            grad_two, stwo_hat, stwo_scale, slow_gains[2], totals[0], totals[1], slow_count
        ).astype(jnp.bfloat16)
        d_ftwo = norm_back(
            fgrad_two, ftwo_hat, ftwo_scale, fast_gains[1], totals[2], totals[3], fast_count
        ).astype(jnp.bfloat16)
        weight_acc[2] = weight_acc[2] + space_weight(act_one, d_two)
        weight_acc[6] = weight_acc[6] + space_weight(fact_one, d_ftwo)
        grad_one = smooth_back(sone_norm, space_back(d_two, slow_space))
        fgrad_one = smooth_back(fone_norm, space_back(d_ftwo, fast_space))
        sums_a = local_sums(grad_one, sone_hat)
        sums_c = local_sums(fgrad_one, fone_hat)
        totals = grad_totals([sums_a[0], sums_a[1], sums_c[0], sums_c[1]])
        slow_gain_acc[1] = slow_gain_acc[1] + totals[1]
        slow_bias_acc[1] = slow_bias_acc[1] + totals[0]
        fast_gain_acc[0] = fast_gain_acc[0] + totals[3]
        fast_bias_acc[0] = fast_bias_acc[0] + totals[2]
        d_one = norm_back(
            grad_one, sone_hat, sone_scale, slow_gains[1], totals[0], totals[1], slow_count
        ).astype(jnp.bfloat16)
        d_fone = norm_back(
            fgrad_one, fone_hat, fone_scale, fast_gains[0], totals[2], totals[3], fast_count
        ).astype(jnp.bfloat16)
        grad_edges = jnp.stack([d_one[0] * slow_mask[0], d_one[-1]], 0)
        grad_rim = padded_2(grad_edges, ((("path", "dp"), 0),), 1)
        back_before = jnp.concatenate([grad_rim[0][None], d_one[:-1]], 0) * slow_mask
        back_after = jnp.concatenate([d_one[1:] * slow_mask[1:], grad_rim[3][None]], 0)
        joined_grad = (
            matmul(back_after, slow_time[0].T)
            + matmul(d_one, slow_time[1].T)
            + matmul(back_before, slow_time[2].T)
            + matmul(d_short, projection.T)
        )
        weight_acc[1] = weight_acc[1] + jnp.stack(
            [
                weight_term(slow_before, d_one),
                weight_term(joined, d_one),
                weight_term(slow_after, d_one),
            ],
            0,
        )
        weight_acc[4] = weight_acc[4] + weight_term(joined, d_short)
        slow_grads_out.append(joined_grad[..., :CS].astype(jnp.bfloat16))
        lat_grad = smooth_back(lat_norm, joined_grad[..., CS:])
        sums_a = local_sums(lat_grad, lat_hat)
        totals = grad_totals([sums_a[0], sums_a[1]])
        slow_gain_acc[0] = slow_gain_acc[0] + totals[1]
        slow_bias_acc[0] = slow_bias_acc[0] + totals[0]
        d_lat = norm_back(
            lat_grad, lat_hat, lat_scale, slow_gains[0], totals[0], totals[1], slow_count
        ).astype(jnp.bfloat16)
        weight_acc[0] = weight_acc[0] + jnp.stack(
            [weight_term(third, d_lat), weight_term(fourth, d_lat)]
            + [weight_term(quads[:, tap_num], d_lat) for tap_num in range(3)],
            0,
        )
        weight_acc[5] = weight_acc[5] + jnp.stack(
            [
                weight_term(fast_before, d_fone),
                weight_term(fast_block, d_fone),
                weight_term(fast_after, d_fone),
            ],
            0,
        )
        blank_grad = jnp.zeros_like(d_fone[:1])
        fback_before = jnp.concatenate([blank_grad, d_fone[:-1]], 0) * fast_mask
        fback_after = jnp.concatenate([d_fone[1:] * fast_mask[1:], blank_grad], 0)
        time_term = (
            matmul(fback_after, fast_time[0].T)
            + matmul(d_fone, fast_time[1].T)
            + matmul(fback_before, fast_time[2].T)
        )
        masked_lat = d_lat * slow_mask
        lat_second = matmul(masked_lat, lateral[0].T)
        lat_first = matmul(masked_lat, lateral[1].T)
        blank_quad = jnp.zeros_like(lat_second[:1])
        quad_zero = matmul(d_lat, lateral[2].T)
        quad_one = matmul(d_lat, lateral[3].T)
        quad_two = matmul(d_lat, lateral[4].T) + jnp.concatenate([lat_second[1:], blank_quad], 0)
        quad_three = jnp.concatenate([lat_first[1:], blank_quad], 0)
        lat_term = jnp.stack([quad_zero, quad_one, quad_two, quad_three], 1).reshape(
            time_term.shape
        )
        first_down = matmul((d_fone[0] * fast_mask[0])[None], fast_time[0].T)[0]
        last_up = matmul(d_fone[-1][None], fast_time[2].T)[0]
        packets = jnp.stack(
            [lat_second[0], lat_first[0] + first_down, jnp.zeros_like(last_up), last_up], 0
        )
        packet_rim = padded_2(packets.astype(jnp.bfloat16), ((("path", "dp"), 0),), 2).astype(
            packets.dtype
        )
        fast_in_total = fast_grad + time_term + lat_term
        fast_in_total = fast_in_total.at[0].add(fast_mask[0].astype(jnp.float32) * packet_rim[1])
        fast_in_total = fast_in_total.at[-2].add(packet_rim[6])
        fast_in_total = fast_in_total.at[-1].add(packet_rim[7])
        fast_grads_out.append(fast_in_total.astype(jnp.bfloat16))
    shards = (
        lax.psum_scatter(
            weight_acc[0].reshape(-1), ("path", "dp"), scatter_dimension=0, tiled=True
        ),
        lax.psum_scatter(
            weight_acc[1].reshape(-1), ("path", "dp"), scatter_dimension=0, tiled=True
        ),
        lax.psum_scatter(
            weight_acc[2].reshape(-1), ("path", "dp"), scatter_dimension=0, tiled=True
        ),
        lax.psum_scatter(
            weight_acc[3].reshape(-1), ("path", "dp"), scatter_dimension=0, tiled=True
        ),
        lax.psum_scatter(
            weight_acc[4].reshape(-1), ("path", "dp"), scatter_dimension=0, tiled=True
        ),
        lax.psum_scatter(
            weight_acc[5].reshape(-1), ("path", "dp"), scatter_dimension=0, tiled=True
        ),
        lax.psum_scatter(
            weight_acc[6].reshape(-1), ("path", "dp"), scatter_dimension=0, tiled=True
        ),
        lax.psum_scatter(
            weight_acc[7].reshape(-1), ("path", "dp"), scatter_dimension=0, tiled=True
        ),
    )
    share_len = slow_gain.shape[0]
    share_start = lax.axis_index(("path", "dp")) * share_len
    slow_gain_grad = lax.dynamic_slice_in_dim(
        jnp.concatenate(slow_gain_acc), share_start, share_len
    )
    slow_bias_grad = lax.dynamic_slice_in_dim(
        jnp.concatenate(slow_bias_acc), share_start, share_len
    )
    return (
        jnp.stack(slow_outs, 0),
        jnp.stack(fast_outs, 0),
        jnp.stack(slow_grads_out, 0),
        jnp.stack(fast_grads_out, 0),
        shards[0],
        shards[1],
        shards[2],
        shards[3],
        shards[4],
        shards[5],
        shards[6],
        shards[7],
        slow_gain_grad,
        slow_bias_grad,
        jnp.concatenate(fast_gain_acc),
        jnp.concatenate(fast_bias_acc),
    )


def solution(mesh):
    placed = (
        P(None, ("path", "dp"), None, None),
        P(None, ("path", "dp"), None, None),
        P(None, ("path", "dp")),
        P(("path", "dp")),
        P(("path", "dp")),
        P(("path", "dp")),
        P(("path", "dp")),
        P(("path", "dp")),
        P(("path", "dp")),
        P(("path", "dp")),
        P(("path", "dp")),
        P(("path", "dp")),
        P(("path", "dp")),
        P(),
        P(),
        P(None, ("path", "dp"), None, None),
        P(None, ("path", "dp"), None, None),
    )
    return jax.shard_map(
        local,
        mesh=mesh,
        in_specs=placed,
        out_specs=(
            P(None, ("path", "dp"), None, None),
            P(None, ("path", "dp"), None, None),
            P(None, ("path", "dp"), None, None),
            P(None, ("path", "dp"), None, None),
            P(("path", "dp")),
            P(("path", "dp")),
            P(("path", "dp")),
            P(("path", "dp")),
            P(("path", "dp")),
            P(("path", "dp")),
            P(("path", "dp")),
            P(("path", "dp")),
            P(("path", "dp")),
            P(("path", "dp")),
            P(),
            P(),
        ),
        check_vma=False,
    )
```

profile of v0, /device:TPU:0, one launch (start us, length us, event | category | flops | bytes accessed | tf_op | source)
XLA Modules:
  0.0 1650.2 jit_solution(3858753073782618247)
XLA Ops:
  11.6 5.5 collective-permute-start
  30.6 43.7 %all-reduce.40 = (bf16[2816]{0:T(1024)(128)(2,1)S(1)}, bf16[2816]{0:T(1024)(128)(2,1)S(1)}, bf16[9216]{0:T(1024)(128)(2,1)S(1)}) all-reduce(bf16[2816]{0:T(1024)(128)(2,1)S(1)} %dynamic-update-slice.19, bf16[2816]{0:T(1024)(128)(2,1)S(1)} %dynamic-update-slice.18, ...), channel_id=1, replica_groups=mesh['path'=2,'dp'=16] {'path','dp'}, use_global_device_ids=true, to_apply=%add.21 | all-reduce | flops 14848 | bytes 59392
  79.9 67.8 %all_gather.20 = bf16[163840]{0:T(1024)(128)(2,1)S(1)} all-gather(bf16[5120]{0:T(1024)(128)(2,1)S(1)} %copy-done.347), channel_id=1, replica_groups=mesh['path'=2,'dp'=16] {'path','dp'}, dimensions={0}, use_global_device_ids=true | all-gather | bytes 337920 | tf_op jit(solution)/shard_map/all_gather | solution.py:185
  156.6 63.8 %all-gather = bf16[32,1,384]{2,1,0:T(2,128)(2,1)S(1)} all-gather(bf16[1,1,384]{2,1,0:T(2,128)(2,1)S(1)} %reshape.1481), channel_id=1, replica_groups=mesh['path'=2,'dp'=16] {'path','dp'}, dimensions={0}, use_global_device_ids=true | all-gather | bytes 25344 | tf_op jit(solution)/shard_map/all_gather | solution.py:190
  236.2 73.4 %all_gather.29 = bf16[262144]{0:T(1024)(128)(2,1)} all-gather(bf16[8192]{0:T(1024)(128)(2,1)} %param.35), channel_id=1, replica_groups=mesh['path'=2,'dp'=16] {'path','dp'}, dimensions={0}, use_global_device_ids=true | all-gather | bytes 540672 | tf_op jit(solution)/shard_map/all_gather | solution.py:188
  311.6 63.4 %all-gather.1 = bf16[32,1,128]{2,1,0:T(2,128)(2,1)S(1)} all-gather(bf16[1,1,128]{2,1,0:T(2,128)(2,1)} %bitcast.1110), channel_id=1, replica_groups=mesh['path'=2,'dp'=16] {'path','dp'}, dimensions={0}, use_global_device_ids=true | all-gather | bytes 8448 | tf_op jit(solution)/shard_map/all_gather | solution.py:192
  375.6 4.8 fusion.500
  410.4 39.4 %all-reduce.38 = (f32[576]{0:T(1024)S(1)}, f32[576]{0:T(1024)S(1)}) all-reduce(f32[576]{0:T(1024)S(1)} %pad_maximum_fusion.28, f32[576]{0:T(1024)S(1)} %pad_maximum_fusion.26), channel_id=1, replica_groups=mesh['path'=2,'dp'=16] {'path','dp'}, use_global_device_ids=true, to_apply=%region_24.25 | all-reduce | flops 1152 | bytes 9216 | tf_op jit(solution)/shard_map/psum | solution.py:97
  458.0 5.6 collective-permute-start.6
  467.2 5.7 pad_slice_fusion.36
  477.8 5.5 collective-permute-start.2
  485.8 5.4 pad_slice_fusion.44
  621.3 5.4 reshape.1497
  626.7 6.6 multiply_reduce_fusion.7
  633.3 4.6 multiply_reduce_fusion.5
  640.1 43.5 %all-reduce.37 = (f32[2624]{0:T(1024)}, f32[2624]{0:T(1024)}) all-reduce(f32[2624]{0:T(1024)S(1)} %concatenate.191, f32[2624]{0:T(1024)} %concatenate.180), channel_id=1, replica_groups=mesh['path'=2,'dp'=16] {'path','dp'}, use_global_device_ids=true, to_apply=%region_31.32 | all-reduce | flops 5248 | bytes 41984 | tf_op jit(solution)/shard_map/psum | solution.py:97
  705.1 41.2 %all-reduce.36 = (f32[768]{0:T(1024)S(1)}, f32[768]{0:T(1024)S(1)}) all-reduce(f32[768]{0:T(1024)S(1)} %pad_maximum_fusion.29, f32[768]{0:T(1024)S(1)} %pad_maximum_fusion.27), channel_id=1, replica_groups=mesh['path'=2,'dp'=16] {'path','dp'}, use_global_device_ids=true, to_apply=%region_36.37 | all-reduce | flops 1536 | bytes 12288 | tf_op jit(solution)/shard_map/psum | solution.py:97
  753.9 39.8 %all-reduce.35 = (f32[2048]{0:T(1024)S(1)}, f32[2048]{0:T(1024)S(1)}) all-reduce(f32[2048]{0:T(1024)S(1)} %pad_maximum_fusion.25, f32[2048]{0:T(1024)S(1)} %pad_maximum_fusion.24), channel_id=1, replica_groups=mesh['path'=2,'dp'=16] {'path','dp'}, use_global_device_ids=true, to_apply=%region_39.40 | all-reduce | flops 4096 | bytes 32768 | tf_op jit(solution)/shard_map/psum | solution.py:97
  794.0 13.5 multiply_reduce_fusion.2
  807.6 5.3 multiply_reduce_fusion.9
  813.0 41.2 %all-reduce.34 = (f32[4352]{0:T(1024)S(1)}, f32[4352]{0:T(1024)S(1)}) all-reduce(f32[4352]{0:T(1024)S(1)} %constant_dynamic-update-slice_fusion.17, f32[4352]{0:T(1024)S(1)} %constant_dynamic-update-slice_fusion.16), channel_id=1, replica_groups=mesh['path'=2,'dp'=16] {'path','dp'}, use_global_device_ids=true, to_apply=%region_61.62 | all-reduce | flops 8704 | bytes 69632 | tf_op jit(solution)/shard_map/psum | solution.py:111
  854.8 6.7 multiply_convert_fusion.1
  875.9 39.8 %all-reduce.33 = (f32[576]{0:T(1024)S(1)}, f32[576]{0:T(1024)S(1)}) all-reduce(f32[576]{0:T(1024)S(1)} %pad_maximum_fusion.32, f32[576]{0:T(1024)S(1)} %pad_maximum_fusion.30), channel_id=1, replica_groups=mesh['path'=2,'dp'=16] {'path','dp'}, use_global_device_ids=true, to_apply=%region_66.67 | all-reduce | flops 1152 | bytes 9216 | tf_op jit(solution)/shard_map/psum | solution.py:111
  925.2 5.0 pad_slice_fusion.20
  966.8 40.7 %all-reduce.32 = (f32[576]{0:T(1024)S(1)}, f32[576]{0:T(1024)S(1)}) all-reduce(f32[576]{0:T(1024)S(1)} %pad_maximum_fusion.33, f32[576]{0:T(1024)S(1)} %pad_maximum_fusion.31), channel_id=1, replica_groups=mesh['path'=2,'dp'=16] {'path','dp'}, use_global_device_ids=true, to_apply=%region_71.72 | all-reduce | flops 1152 | bytes 9216 | tf_op jit(solution)/shard_map/psum | solution.py:111
  1075.1 5.1 fusion.467
  1091.2 4.9 collective-permute-start.11
  1097.4 5.2 collective-permute-start.9
  1134.5 5.2 collective-permute-start.14
  1214.1 5.2 fusion
  1252.6 116.4 %all-reduce.44.cloned.1.call-done = (f32[512]{0:T(512)}, f32[512]{0:T(512)}, f32[12288]{0:T(1024)}, f32[9216]{0:T(1024)}, f32[4096]{0:T(1024)}) async-done(((f32[512]{0:T(512)}, f32[512]{0:T(512)}, f32[12288]{0:T(1024)}, f32[9216]{0:T(1024)}, f32[4096]{0:T(1024)}), (f32[512]{0:T(512)}, f32[512]{0:T(512)}, f32[12288]{0:T(1024)}, f32[9216]{0:T(1024)}, f32[4096]{0:T(1024)})) %all-reduce.44.cloned.1.call-update) | async-done | bytes 106512 | tf_op jit(solution)/shard_map/psum | solution.py:111
  1412.4 223.4 %all-reduce.46.cloned.1.call-done = (f32[163840]{0:T(1024)}, f32[983040]{0:T(1024)}, f32[589824]{0:T(1024)}, f32[262144]{0:T(1024)}, f32[1310720]{0:T(1024)}) async-done(((f32[163840]{0:T(1024)}, f32[983040]{0:T(1024)}, f32[589824]{0:T(1024)}, f32[262144]{0:T(1024)}, f32[1310720]{0:T(1024)}), (f32[163840]{0:T(1024)}, f32[983040]{0:T(1024)}, f32[589824]{0:T(1024)}, f32[262144]{0:T(1024)}, ...) | async-done | bytes 13238288
  (1528 shorter events, 587.1 us)
Async XLA Ops:
  7.2 569.4 %all-gather.10.cloned.1.call-start = ((), (), s32[]{:S(2)}) async-start(), calls=%async_computation.2 | async-start | bytes 1216512 | tf_op jit(solution)/shard_map/all_gather | solution.py:187
  7.9 590.0 %all-gather.6.cloned.1.call-start = ((), (), s32[]{:S(2)}) async-start(), calls=%async_computation | async-start | bytes 2027520 | tf_op jit(solution)/shard_map/all_gather | solution.py:186
  8.7 612.6 %all-gather.8.cloned.1.call-start = ((), (), s32[]{:S(2)}) async-start(), calls=%async_computation.1 | async-start | bytes 2703360 | tf_op jit(solution)/shard_map/all_gather | solution.py:189
  11.6 383.7 %collective-permute-start = (bf16[2,196,128]{2,1,0:T(8,128)(2,1)}, bf16[2,196,128]{2,1,0:T(8,128)(2,1)}, u32[]{:S(2)}, u32[]{:S(2)}) collective-permute-start(bf16[2,196,128]{2,1,0:T(8,128)(2,1)} %pad_maximum_fusion.20), channel_id=1, source_target_pairs={{0,1},{1,2},{2,3},{3,4},{4,5},{5,6},{6,7},{7,8},{8,9},{9,10},{10,1... | collective-permute-start | bytes 301064 | tf_op jit(solution)/shard_map/ppermute | solution.py:26
  17.7 376.6 %collective-permute-start.4 = (bf16[2,196,128]{2,1,0:T(8,128)(2,1)}, bf16[2,196,128]{2,1,0:T(8,128)(2,1)}, u32[]{:S(2)}, u32[]{:S(2)}) collective-permute-start(bf16[2,196,128]{2,1,0:T(8,128)(2,1)} %pad_maximum_fusion.21), channel_id=1, source_target_pairs={{0,1},{1,2},{2,3},{3,4},{4,5},{5,6},{6,7},{7,8},{8,9},{9,10},{10,1... | collective-permute-start | bytes 301064 | tf_op jit(solution)/shard_map/ppermute | solution.py:26
  21.6 203.8 %copy-start.323 = (bf16[4]{0:T(256)(128)(2,1)}, bf16[4]{0:T(256)(128)(2,1)S(1)}, u32[]{:S(2)}) copy-start(bf16[4]{0:T(256)(128)(2,1)S(1)} %get-tuple-element.534) | copy-start | bytes 28
  21.8 128.6 %copy-start.359 = (bf16[16]{0:T(256)(128)(2,1)}, bf16[16]{0:T(256)(128)(2,1)S(1)}, u32[]{:S(2)}) copy-start(bf16[16]{0:T(256)(128)(2,1)S(1)} %fusion.428) | copy-start | bytes 100
  22.5 383.0 %collective-permute-start.5 = (bf16[2,196,128]{2,1,0:T(8,128)(2,1)}, bf16[2,196,128]{2,1,0:T(8,128)(2,1)}, u32[]{:S(2)}, u32[]{:S(2)}) collective-permute-start(bf16[2,196,128]{2,1,0:T(8,128)(2,1)} %stack.298), channel_id=1, source_target_pairs={{1,0},{2,1},{3,2},{4,3},{5,4},{6,5},{7,6},{8,7},{9,8},{10,9},{11,1... | collective-permute-start | bytes 301064 | tf_op jit(solution)/shard_map/ppermute | solution.py:28
  24.7 383.2 %collective-permute-start.1 = (bf16[2,196,128]{2,1,0:T(8,128)(2,1)}, bf16[2,196,128]{2,1,0:T(8,128)(2,1)}, u32[]{:S(2)}, u32[]{:S(2)}) collective-permute-start(bf16[2,196,128]{2,1,0:T(8,128)(2,1)} %stack.295), channel_id=1, source_target_pairs={{1,0},{2,1},{3,2},{4,3},{5,4},{6,5},{7,6},{8,7},{9,8},{10,9},{11,1... | collective-permute-start | bytes 301064 | tf_op jit(solution)/shard_map/ppermute | solution.py:28
  26.0 1343.0 %all-reduce.44.cloned.1.call-start = ((), (), s32[]{:S(2)}) async-start(), calls=%async_computation.3 | async-start | bytes 212992 | tf_op jit(solution)/shard_map/psum | solution.py:111
  26.4 127.0 %copy-start.16 = (bf16[1,16,196,128]{3,1,2,0:T(8,128)(2,1)}, bf16[1,16,196,128]{3,1,2,0:T(8,128)(2,1)S(1)}, u32[]{:S(2)}) copy-start(bf16[1,16,196,128]{3,1,2,0:T(8,128)(2,1)S(1)} %get-tuple-element.295) | copy-start | bytes 2408452
  156.5 241.8 %copy-start.199 = (bf16[128,256,1]{1,0,2:T(8,128)(2,1)}, bf16[128,256,1]{1,0,2:T(8,128)(2,1)S(1)}, u32[]{:S(2)}) copy-start(bf16[128,256,1]{1,0,2:T(8,128)(2,1)S(1)} %reshape.1488) | copy-start | bytes 196612
  156.5 242.6 %copy-start.202 = (bf16[128,256,1]{1,0,2:T(8,128)(2,1)}, bf16[128,256,1]{1,0,2:T(8,128)(2,1)S(1)}, u32[]{:S(2)}) copy-start(bf16[128,256,1]{1,0,2:T(8,128)(2,1)S(1)} %reshape.1489) | copy-start | bytes 196612
  156.6 244.0 %copy-start.189 = (bf16[128,256,1]{1,0,2:T(8,128)(2,1)}, bf16[128,256,1]{1,0,2:T(8,128)(2,1)S(1)}, u32[]{:S(2)}) copy-start(bf16[128,256,1]{1,0,2:T(8,128)(2,1)S(1)} %reshape.1490) | copy-start | bytes 196612
  220.6 182.7 %copy-start.210 = (bf16[128,32]{1,0:T(8,128)(2,1)}, bf16[128,32]{1,0:T(8,128)(2,1)S(1)}, u32[]{:S(2)}) copy-start(bf16[128,32]{1,0:T(8,128)(2,1)S(1)} %slice.1530) | copy-start | bytes 24580
  221.4 187.3 %copy-start.207 = (bf16[128,32]{1,0:T(8,128)(2,1)}, bf16[128,32]{1,0:T(8,128)(2,1)S(1)}, u32[]{:S(2)}) copy-start(bf16[128,32]{1,0:T(8,128)(2,1)S(1)} %slice.1540) | copy-start | bytes 24580
  454.1 155.7 %collective-permute-start.7 = (bf16[1,196,1280]{2,1,0:T(8,128)(2,1)}, bf16[1,196,1280]{2,1,0:T(8,128)(2,1)}, u32[]{:S(2)}, u32[]{:S(2)}) collective-permute-start(bf16[1,196,1280]{2,1,0:T(8,128)(2,1)} %get-tuple-element.276), channel_id=1, source_target_pairs={{1,0},{2,1},{3,2},{4,3},{5,4},{6,5},{7,6},{8,7},{9,8},{10,9},{11,1... | collective-permute-start | bytes 1505288 | tf_op jit(solution)/shard_map/ppermute | solution.py:28
  458.0 156.5 %collective-permute-start.6 = (bf16[1,196,1280]{2,1,0:T(8,128)(2,1)}, bf16[1,196,1280]{2,1,0:T(8,128)(2,1)}, u32[]{:S(2)}, u32[]{:S(2)}) collective-permute-start(bf16[1,196,1280]{2,1,0:T(8,128)(2,1)} %get-tuple-element.275), channel_id=1, source_target_pairs={{0,1},{1,2},{2,3},{3,4},{4,5},{5,6},{6,7},{7,8},{8,9},{9,10},{10,1... | collective-permute-start | bytes 1505288 | tf_op jit(solution)/shard_map/ppermute | solution.py:26
  474.1 138.5 %collective-permute-start.3 = (bf16[1,196,1280]{2,1,0:T(8,128)(2,1)}, bf16[1,196,1280]{2,1,0:T(8,128)(2,1)}, u32[]{:S(2)}, u32[]{:S(2)}) collective-permute-start(bf16[1,196,1280]{2,1,0:T(8,128)(2,1)} %get-tuple-element.272), channel_id=1, source_target_pairs={{1,0},{2,1},{3,2},{4,3},{5,4},{6,5},{7,6},{8,7},{9,8},{10,9},{11,1... | collective-permute-start | bytes 1505288 | tf_op jit(solution)/shard_map/ppermute | solution.py:28
  477.8 140.2 %collective-permute-start.2 = (bf16[1,196,1280]{2,1,0:T(8,128)(2,1)}, bf16[1,196,1280]{2,1,0:T(8,128)(2,1)}, u32[]{:S(2)}, u32[]{:S(2)}) collective-permute-start(bf16[1,196,1280]{2,1,0:T(8,128)(2,1)} %get-tuple-element.271), channel_id=1, source_target_pairs={{0,1},{1,2},{2,3},{3,4},{4,5},{5,6},{6,7},{7,8},{8,9},{9,10},{10,1... | collective-permute-start | bytes 1505288 | tf_op jit(solution)/shard_map/ppermute | solution.py:26
  746.3 170.7 %copy-start.399 = (f32[256]{0:T(256)}, f32[256]{0:T(256)S(1)}, u32[]{:S(2)}) copy-start(f32[256]{0:T(256)S(1)} %get-tuple-element.501) | copy-start | bytes 3076
  746.3 170.7 %copy-start.401 = (f32[256]{0:T(256)}, f32[256]{0:T(256)S(1)}, u32[]{:S(2)}) copy-start(f32[256]{0:T(256)S(1)} %get-tuple-element.502) | copy-start | bytes 3076
  746.4 127.3 %copy-start.390 = (f32[256]{0:T(256)}, f32[256]{0:T(256)S(1)}, u32[]{:S(2)}) copy-start(f32[256]{0:T(256)S(1)} %add_rsqrt_fusion.2) | copy-start | bytes 3076
  1091.2 133.2 %collective-permute-start.11 = (bf16[1,196,256]{2,1,0:T(8,128)(2,1)}, bf16[1,196,256]{2,1,0:T(8,128)(2,1)}, u32[]{:S(2)}, u32[]{:S(2)}) collective-permute-start(bf16[1,196,256]{2,1,0:T(8,128)(2,1)} %get-tuple-element.354), channel_id=1, source_target_pairs={{0,1},{1,2},{2,3},{3,4},{4,5},{5,6},{6,7},{7,8},{8,9},{9,10},{10,1... | collective-permute-start | bytes 301064 | tf_op jit(solution)/shard_map/ppermute | solution.py:26
  1096.1 133.5 %collective-permute-start.10 = (bf16[1,196,256]{2,1,0:T(8,128)(2,1)}, bf16[1,196,256]{2,1,0:T(8,128)(2,1)}, u32[]{:S(2)}, u32[]{:S(2)}) collective-permute-start(bf16[1,196,256]{2,1,0:T(8,128)(2,1)} %get-tuple-element.353), channel_id=1, source_target_pairs={{1,0},{2,1},{3,2},{4,3},{5,4},{6,5},{7,6},{8,7},{9,8},{10,9},{11,1... | collective-permute-start | bytes 301064 | tf_op jit(solution)/shard_map/ppermute | solution.py:28
  1097.4 136.1 %collective-permute-start.9 = (bf16[1,196,256]{2,1,0:T(8,128)(2,1)}, bf16[1,196,256]{2,1,0:T(8,128)(2,1)}, u32[]{:S(2)}, u32[]{:S(2)}) collective-permute-start(bf16[1,196,256]{2,1,0:T(8,128)(2,1)} %get-tuple-element.350), channel_id=1, source_target_pairs={{0,1},{1,2},{2,3},{3,4},{4,5},{5,6},{6,7},{7,8},{8,9},{9,10},{10,1... | collective-permute-start | bytes 301064 | tf_op jit(solution)/shard_map/ppermute | solution.py:26
  1102.6 132.9 %collective-permute-start.8 = (bf16[1,196,256]{2,1,0:T(8,128)(2,1)}, bf16[1,196,256]{2,1,0:T(8,128)(2,1)}, u32[]{:S(2)}, u32[]{:S(2)}) collective-permute-start(bf16[1,196,256]{2,1,0:T(8,128)(2,1)} %get-tuple-element.349), channel_id=1, source_target_pairs={{1,0},{2,1},{3,2},{4,3},{5,4},{6,5},{7,6},{8,7},{9,8},{10,9},{11,1... | collective-permute-start | bytes 301064 | tf_op jit(solution)/shard_map/ppermute | solution.py:28
  1134.5 111.8 %collective-permute-start.14 = (bf16[2,196,128]{2,1,0:T(8,128)(2,1)}, bf16[2,196,128]{2,1,0:T(8,128)(2,1)}, u32[]{:S(2)}, u32[]{:S(2)}) collective-permute-start(bf16[2,196,128]{2,1,0:T(8,128)(2,1)} %stack.317), channel_id=1, source_target_pairs={{0,1},{1,2},{2,3},{3,4},{4,5},{5,6},{6,7},{7,8},{8,9},{9,10},{10,1... | collective-permute-start | bytes 301064 | tf_op jit(solution)/shard_map/ppermute | solution.py:26
  1224.4 23.4 %collective-permute-start.12 = (bf16[2,196,128]{2,1,0:T(8,128)(2,1)S(1)}, bf16[2,196,128]{2,1,0:T(8,128)(2,1)S(1)}, u32[]{:S(2)}, u32[]{:S(2)}) collective-permute-start(bf16[2,196,128]{2,1,0:T(8,128)(2,1)S(1)} %stack.310), channel_id=1, source_target_pairs={{0,1},{1,2},{2,3},{3,4},{4,5},{5,6},{6,7},{7,8},{8,9},{9,10},{10,1... | collective-permute-start | bytes 301064 | tf_op jit(solution)/shard_map/ppermute | solution.py:26
  1243.7 392.1 %all-reduce.46.cloned.1.call-start = ((), (), s32[]{:S(2)}) async-start(), calls=%async_computation.4 | async-start | bytes 26476544
  1391.6 17.8 %collective-permute-start.15 = (bf16[2,196,128]{2,1,0:T(8,128)(2,1)}, bf16[2,196,128]{2,1,0:T(8,128)(2,1)}, u32[]{:S(2)}, u32[]{:S(2)}) collective-permute-start(bf16[2,196,128]{2,1,0:T(8,128)(2,1)} %pad_maximum_fusion.23), channel_id=1, source_target_pairs={{1,0},{2,1},{3,2},{4,3},{5,4},{6,5},{7,6},{8,7},{9,8},{10,9},{11,1... | collective-permute-start | bytes 301064 | tf_op jit(solution)/shard_map/ppermute | solution.py:28
  1399.1 11.3 collective-permute-start.13
  (460 other events, 3719.5 us)
Sparse Core Ops, SparseCore 0:
  10.9 56.7 all-gather.9
  70.6 55.8 all-gather.5
  129.3 56.9 all-gather.7
  1243.8 125.1 all-reduce.43
  1391.0 244.7 all-reduce.45
where the time goes:
time: 1660 us; the launch traced here: 1650 us
  blocking collectives  598 us (36%)
  waiting for transfers between devices  341 us (21%)
  local copies, waits for them, and re-layouts  320 us (19%)
  matrix products  237 us (14%)
  other arithmetic  84.5 us (5%)
  starting transfers between devices  49.5 us (3%)
  between operations  20.5 us (1%)
    unnamed x6, waiting for transfers between devices  225 us
    psum x4, blocking collectives, norm_totals(): joined = lax.psum(jnp.concatenate(firsts + seconds), ('path', 'dp'))  164 us
    dot_general x132, matrix products, matmul(): result = jnp.dot(flat_in, weight, preferred_element_type=jnp.float32)  151 us
    psum x3, blocking collectives, grad_totals(): joined = lax.psum(jnp.concatenate(vectors), ('path', 'dp'))  122 us
    psum x1, waiting for transfers between devices, grad_totals(): joined = lax.psum(jnp.concatenate(vectors), ('path', 'dp'))  116 us
    dot_general x64, matrix products, weight_term(): lax.dot_general(inputs.reshape(-1, inputs.shape[-1]), grads.reshape(-1, g...  85.9 us
    all_gather x1, blocking collectives, local(): lax.all_gather(w_slow_out, ('path', 'dp'), axis=0, tiled=True)  73.4 us
    slice x40, local copies, waits for them, and re-layouts, space_taps(): padded[:, row_at:row_at + HH, col_at:col_at + WW, :].reshape(frames.shape)  72.3 us
  transfers between devices with their start and end apart: 21, of which 2 were waited for; matrix products, arithmetic and copies ran while one was open for 23% of the time, Pallas kernels for 0%

commit v1 on v0

v1 whole, which is shorter than its diff:
```python
import jax
import jax.numpy as jnp
from jax import lax
from jax.sharding import PartitionSpec as P

CS = 1024
CL = 256
CM = 256
CF = 128
CFM = 32
HH = 14
WW = 14
PIX = HH * WW
ROWS = 208
EPS = 1e-05
AXES = ("path", "dp")
BF = jnp.bfloat16
F32 = jnp.float32


def swap(value, bit):
    count = lax.axis_size(AXES)
    return lax.ppermute(value, AXES, [(i, i ^ bit) for i in range(count)])


def dp_bits():
    count = lax.axis_size("dp")
    bits = []
    bit = 1
    while bit < count:
        bits.append(bit)
        bit *= 2
    return bits


def all_sum(value):
    value = value + swap(value, lax.axis_size("dp"))
    bits = dp_bits()
    while bits:
        if len(bits) == 1:
            value = value + swap(value, bits[0])
            bits = []
        else:
            one, two = bits[:2]
            first, second, third = swap(value, one), swap(value, two), swap(value, one + two)
            value = (value + first) + (second + third)
            bits = bits[2:]
    return value


def has_bit(bit):
    return (lax.axis_index(AXES) & bit) != 0


def gather_bits(value, bits):
    for bit in bits:
        other = swap(value, bit)
        value = jnp.where(
            has_bit(bit),
            jnp.concatenate([other, value], 0),
            jnp.concatenate([value, other], 0),
        )
    return value


def gather_small(value):
    return gather_bits(value[None], dp_bits() + [lax.axis_size("dp")])


def scatter_route(value, order):
    places = [lax.axis_size("dp")] + dp_bits()[::-1]
    for bit in order:
        dim = places.index(bit)
        low = lax.index_in_dim(value, 0, dim, False)
        high = lax.index_in_dim(value, 1, dim, False)
        mine = has_bit(bit)
        keep = jnp.where(mine, high, low)
        send = jnp.where(mine, low, high).astype(BF)
        value = keep.astype(F32) + swap(send, bit).astype(F32)
        places.remove(bit)
    return value


def scatter_sum(value):
    bits = dp_bits()
    path = lax.axis_size("dp")
    shaped = value.reshape((2,) * (len(bits) + 1) + value.shape[1:])
    low, high = bits[:2], bits[2:][::-1]
    rows = value.shape[1]
    cut = rows // 16 * 8
    if cut == 0:
        return scatter_route(shaped, [path] + low + high)
    one = scatter_route(shaped[..., :cut, :], [path] + low + high)
    two = scatter_route(shaped[..., cut:, :], [path] + low[::-1] + high)
    return jnp.concatenate([one, two], 0)


def from_before(value):
    count = lax.axis_size(AXES)
    return lax.ppermute(value, AXES, [(i, i + 1) for i in range(count - 1)])


def from_after(value):
    count = lax.axis_size(AXES)
    return lax.ppermute(value, AXES, [(i + 1, i) for i in range(count - 1)])


def gelu_parts(value):
    cubic = 0.7978845608028654 * (value + 0.044715 * (value * value * value))
    return jnp.tanh(cubic)


def gelu(value):
    return 0.5 * value * (1.0 + gelu_parts(value))


def gelu_slope(value):
    tan = gelu_parts(value)
    inner = 0.7978845608028654 * (1.0 + (3 * 0.044715) * (value * value))
    return 0.5 * (1.0 + tan) + 0.5 * value * (1.0 - tan * tan) * inner


def dot(left, right):
    return lax.dot_general(
        left, right, (((left.ndim - 1,), (0,)), ((), ())), preferred_element_type=F32
    )


def dot_t(left, right):
    return lax.dot_general(
        left, right, (((left.ndim - 1,), (1,)), ((), ())), preferred_element_type=F32
    )


def outer(left, right):
    return lax.dot_general(
        left.reshape(-1, left.shape[-1]),
        right.reshape(-1, right.shape[-1]),
        (((0,), (0,)), ((), ())),
        preferred_element_type=F32,
    )


def row_masks():
    row = lax.broadcasted_iota(jnp.int32, (1, ROWS, 1), 1)
    col = row % WW
    real = row < PIX
    return dict(
        real=real,
        left=real & (col != 0),
        right=real & (col != WW - 1),
        top=real & (row >= WW),
        bottom=row < PIX - WW,
    )


def roll(value, step, mask):
    return jnp.where(mask, jnp.roll(value, step, 1), 0)


def column_taps(value, masks):
    return jnp.concatenate(
        [roll(value, 1, masks["left"]), value, roll(value, -1, masks["right"])], -1
    )


def in_space(value, weight, masks):
    lanes = value.shape[-1]
    taps = dot(column_taps(value, masks), weight)
    return (
        roll(taps[..., :lanes], WW, masks["top"])
        + taps[..., lanes : 2 * lanes]
        + roll(taps[..., 2 * lanes :], -WW, masks["bottom"])
    )


def row_taps(value, masks):
    return jnp.concatenate(
        [roll(value, -WW, masks["bottom"]), value, roll(value, WW, masks["top"])], -1
    )


def space_back(taps, weight, masks):
    lanes = taps.shape[-1] // 3
    back = dot_t(taps, weight)
    return (
        roll(back[..., :lanes], -1, masks["right"])
        + back[..., lanes : 2 * lanes]
        + roll(back[..., 2 * lanes :], 1, masks["left"])
    )


def pad_rows(value):
    return jnp.pad(value, [(0, 0)] * (value.ndim - 2) + [(0, ROWS - PIX), (0, 0)])


def to_quads(value):
    micro, frames, _, lanes = value.shape
    quads = pad_rows(value).reshape(micro * frames // 4, 4, ROWS, lanes)
    return jnp.concatenate([quads[:, place] for place in range(4)], -1)


def from_quads(value, micro):
    lanes = value.shape[-1] // 4
    parts = [value[:, :PIX, place * lanes : (place + 1) * lanes] for place in range(4)]
    return jnp.stack(parts, 1).reshape(micro, -1, PIX, lanes)


def fold(vector):
    parts = vector.reshape(vector.shape[:-1] + (4, -1))
    return jnp.tile(jnp.sum(parts, -2), 4)


def sums_of(micro, *values):
    return jnp.concatenate(
        [jnp.sum(value.reshape((micro, -1) + value.shape[-1:]), 1) for value in values], -1
    )


def local(
    slow_in,
    fast_in,
    clip_starts,
    w_lateral,
    w_slow_time,
    w_slow_space,
    w_slow_out,
    w_projection,
    w_fast_time,
    w_fast_space,
    w_fast_out,
    slow_gain,
    slow_bias,
    fast_gain,
    fast_bias,
    slow_cotangent,
    fast_cotangent,
):
    devices = lax.axis_size(AXES)
    micro, frames = slow_in.shape[:2]
    groups = micro * frames
    masks = row_masks()
    real = masks["real"]
    slow_count = float(frames * PIX * devices)
    fast_count = 4.0 * slow_count

    edge_down = from_before(fast_in[:, -2:])
    edge_up = from_after(fast_in[:, :1])

    shards = [w_lateral, w_fast_time, w_fast_space, w_fast_out, slow_gain, slow_bias]
    small = jnp.concatenate(shards)
    small = gather_small(jnp.pad(small, (0, -small.shape[0] % 1024)))
    pieces = []
    at = 0
    for shard in shards:
        pieces.append(small[:, at : at + shard.shape[0]].reshape(-1))
        at += shard.shape[0]
    lateral = pieces[0].reshape(5 * CF, CL)
    fast_time = pieces[1].reshape(3, CF, CFM)
    fast_space = pieces[2].reshape(3, 3, CFM, CFM)
    fast_proj = pieces[3].reshape(CFM, CF)
    gains = pieces[4].astype(F32)
    biases = pieces[5].astype(F32)

    def gathered(shard, lanes):
        return lax.all_gather(shard.reshape(-1, lanes), AXES, axis=0, tiled=True)

    slow_time = gathered(w_slow_time, CM)
    slow_time = jnp.concatenate(
        [slow_time[tap * (CS + CL) : (tap + 1) * (CS + CL)] for tap in range(3)], -1
    )
    projection = gathered(w_projection, CS)
    space = gathered(w_slow_space, CM).reshape(3, 3, CM, CM)
    slow_space = jnp.concatenate(
        [jnp.concatenate([space[a, c] for a in range(3)], -1) for c in range(3)], 0
    )
    slow_proj = gathered(w_slow_out, CS)

    band = jnp.stack([jnp.eye(7, 4, -1 - k, dtype=BF) for k in range(3)], 0)
    fast_band = jnp.sum(
        band[:, :, None, :, None] * fast_time[:, None, :, None, :], 0, dtype=F32
    ).astype(BF).reshape(7 * CF, 4 * CFM)
    lat_band = jnp.concatenate([lateral, jnp.zeros((2 * CF, CL), BF)], 0)
    w_first = jnp.concatenate([lat_band, fast_band], -1)
    eye4 = jnp.eye(4, dtype=BF)
    fspace = (
        fast_space.transpose(1, 2, 0, 3)[:, None, :, :, None, :]
        * eye4[None, :, None, None, :, None]
    )
    fspace = fspace.reshape(3 * 4 * CFM, 3 * 4 * CFM)
    fproj = (fast_proj[None, :, None, :] * eye4[:, None, :, None]).reshape(4 * CFM, 4 * CF)

    def cut(vector, start, extent):
        return vector[start : start + extent][None, None]

    places = [(0, CL), (CL, CM), (CL + CM, CM), (CL + 2 * CM, CS), (CL + 2 * CM + CS, CS)]
    sg = [cut(gains, *place) for place in places]
    sb = [cut(biases, *place) for place in places]
    fg_all, fb_all = fast_gain.astype(F32), fast_bias.astype(F32)
    fg = [
        jnp.tile(part, 4)[None, None]
        for part in (fg_all[:CFM], fg_all[CFM : 2 * CFM], fg_all[2 * CFM :])
    ]
    fb = [
        jnp.tile(part, 4)[None, None]
        for part in (fb_all[:CFM], fb_all[CFM : 2 * CFM], fb_all[2 * CFM :])
    ]

    def spread(vector):
        return jnp.repeat(vector, frames, 0)[:, None]

    def split(total, extents):
        out = []
        start = 0
        for extent in extents:
            out.append(total[:, start : start + extent])
            start += extent
        return out

    def hat(value, first, second, count):
        mean = first / count
        scale = lax.rsqrt(second / count - mean * mean + EPS)
        scale = spread(scale)
        return (value - spread(mean)) * scale, scale

    def back(grad, normed, scale, gain, one, two, count):
        value = gain * scale * (grad - spread(one) / count - normed * (spread(two) / count))
        return jnp.where(real, value, 0).astype(BF)

    def shifted(value, edge, link):
        parts = value.reshape((micro, frames) + value.shape[1:])
        parts = jnp.concatenate([edge[:, None].astype(value.dtype), parts[:, :-1]], 1)
        return parts.reshape(value.shape) * link.astype(value.dtype)

    def ahead(value, edge, link):
        parts = value.reshape((micro, frames) + value.shape[1:])
        parts = jnp.concatenate([parts[:, 1:], edge[:, None].astype(value.dtype)], 1)
        return parts.reshape(value.shape) * link.astype(value.dtype)

    link = (1 - clip_starts).astype(F32)
    next_link = jnp.concatenate([link[:, 1:], from_after(link[:, :1])], 1)
    link = link.reshape(groups, 1, 1)
    next_link = next_link.reshape(groups, 1, 1)

    quads = to_quads(fast_in)
    edge_down = pad_rows(edge_down)
    edge_down = jnp.concatenate([edge_down[:, 0], edge_down[:, 1]], -1)
    edge_up = pad_rows(edge_up[:, 0])
    z = jnp.concatenate(
        [
            shifted(quads[..., 2 * CF :], edge_down, link),
            quads,
            ahead(quads[..., :CF], edge_up, next_link),
        ],
        -1,
    )
    first = dot(z, w_first)
    lat_pre, fone = first[..., :CL], first[..., CL:]
    total = all_sum(sums_of(micro, lat_pre, fone, lat_pre * lat_pre, fone * fone))
    s = split(total, [CL, 128, CL, 128])
    lat_hat, lat_scale = hat(lat_pre, s[0], s[2], slow_count)
    fone_hat, fone_scale = hat(fone, fold(s[1]), fold(s[3]), fast_count)

    lat_norm = lat_hat * sg[0] + sb[0]
    lat_act = jnp.where(real, gelu(lat_norm), 0).astype(BF)
    joined = jnp.concatenate([pad_rows(slow_in).reshape(groups, ROWS, CS), lat_act], -1)
    taps = dot(joined, slow_time)
    last = taps.reshape(micro, frames, ROWS, 3 * CM)[:, -1, :, :CM].astype(BF)
    head = taps.reshape(micro, frames, ROWS, 3 * CM)[:, 0, :, 2 * CM :].astype(BF)
    last = from_before(last)
    head = from_after(head)
    short = dot(joined, projection)
    fone_norm = fone_hat * fg[0] + fb[0]
    fact_one = jnp.where(real, gelu(fone_norm), 0).astype(BF)
    ftwo = in_space(fact_one, fspace, masks)
    slow_one = (
        shifted(taps[..., :CM], last, link)
        + taps[..., CM : 2 * CM]
        + ahead(taps[..., 2 * CM :], head, next_link)
    )
    total = all_sum(
        sums_of(micro, slow_one, short, ftwo, slow_one * slow_one, short * short, ftwo * ftwo)
    )
    s = split(total, [CM, CS, 128, CM, CS, 128])
    one_hat, one_scale = hat(slow_one, s[0], s[3], slow_count)
    short_hat, short_scale = hat(short, s[1], s[4], slow_count)
    ftwo_hat, ftwo_scale = hat(ftwo, fold(s[2]), fold(s[5]), fast_count)

    one_norm = one_hat * sg[1] + sb[1]
    act_one = jnp.where(real, gelu(one_norm), 0).astype(BF)
    slow_two = in_space(act_one, slow_space, masks)
    ftwo_norm = ftwo_hat * fg[1] + fb[1]
    fact_two = jnp.where(real, gelu(ftwo_norm), 0).astype(BF)
    fthree = dot(fact_two, fproj)
    total = all_sum(sums_of(micro, slow_two, fthree, slow_two * slow_two, fthree * fthree))
    s = split(total, [CM, 512, CM, 512])
    two_hat, two_scale = hat(slow_two, s[0], s[2], slow_count)
    fthree_hat, fthree_scale = hat(fthree, fold(s[1]), fold(s[3]), fast_count)

    two_norm = two_hat * sg[2] + sb[2]
    act_two = jnp.where(real, gelu(two_norm), 0).astype(BF)
    slow_three = dot(act_two, slow_proj)
    total = all_sum(sums_of(micro, slow_three, slow_three * slow_three))
    s = split(total, [CS, CS])
    three_hat, three_scale = hat(slow_three, s[0], s[1], slow_count)

    fast_total = fthree_hat * fg[2] + fb[2] + quads.astype(F32)
    fast_out = from_quads(gelu(fast_total).astype(BF), micro)
    fast_grad = gelu_slope(fast_total) * to_quads(fast_cotangent).astype(F32)
    slow_total = three_hat * sg[3] + sb[3] + (short_hat * sg[4] + sb[4])
    slow_out = gelu(slow_total).astype(BF)[:, :PIX].reshape(slow_in.shape)
    slow_grad = gelu_slope(slow_total) * pad_rows(slow_cotangent).reshape(
        groups, ROWS, CS
    ).astype(F32)
    total = all_sum(
        sums_of(
            micro,
            slow_grad,
            slow_grad * three_hat,
            slow_grad * short_hat,
            fast_grad,
            fast_grad * fthree_hat,
        )
    )
    s = split(total, [CS, CS, CS, 512, 512])
    sum_a = s
    d_three = back(slow_grad, three_hat, three_scale, sg[3], s[0], s[1], slow_count)
    d_short = back(slow_grad, short_hat, short_scale, sg[4], s[0], s[2], slow_count)
    d_fthree = back(
        fast_grad, fthree_hat, fthree_scale, fg[2], fold(s[3]), fold(s[4]), fast_count
    )

    grad_two = gelu_slope(two_norm) * dot_t(d_three, slow_proj)
    fgrad_two = gelu_slope(ftwo_norm) * dot_t(d_fthree, fproj)
    total = all_sum(sums_of(micro, grad_two, grad_two * two_hat, fgrad_two, fgrad_two * ftwo_hat))
    s = split(total, [CM, CM, 128, 128])
    sum_b = s
    d_two = back(grad_two, two_hat, two_scale, sg[2], s[0], s[1], slow_count)
    d_ftwo = back(fgrad_two, ftwo_hat, ftwo_scale, fg[1], fold(s[2]), fold(s[3]), fast_count)
    out_grad = outer(act_two, d_three)
    fout_grad = outer(fact_two, d_fthree)
    proj_grad = outer(joined, d_short)

    two_taps = row_taps(d_two, masks)
    ftwo_taps = row_taps(d_ftwo, masks)
    grad_one = gelu_slope(one_norm) * space_back(two_taps, slow_space, masks)
    fgrad_one = gelu_slope(fone_norm) * space_back(ftwo_taps, fspace, masks)
    total = all_sum(sums_of(micro, grad_one, grad_one * one_hat, fgrad_one, fgrad_one * fone_hat))
    s = split(total, [CM, CM, 128, 128])
    sum_c = s
    d_one = back(grad_one, one_hat, one_scale, sg[1], s[0], s[1], slow_count)
    d_fone = back(fgrad_one, fone_hat, fone_scale, fg[0], fold(s[2]), fold(s[3]), fast_count)
    space_grad = outer(column_taps(act_one, masks), two_taps)
    fspace_grad = outer(column_taps(fact_one, masks), ftwo_taps)

    ends = jnp.concatenate([d_one, d_fone], -1).reshape(micro, frames, ROWS, CM + 128)
    before = from_before(ends[:, -1])
    after = from_after(ends[:, 0])
    trio = jnp.concatenate(
        [
            ahead(d_one, after[..., :CM], next_link),
            d_one,
            shifted(d_one, before[..., :CM], link),
        ],
        -1,
    )
    joined_grad = dot_t(trio, slow_time) + dot_t(d_short, projection)
    time_grad = outer(joined, trio)
    slow_in_grad = joined_grad[:, :PIX, :CS].astype(BF).reshape(slow_in.shape)
    lat_grad = gelu_slope(lat_norm) * joined_grad[..., CS:]
    total = all_sum(sums_of(micro, lat_grad, lat_grad * lat_hat))
    s = split(total, [CL, CL])
    sum_d = s
    d_lat = back(lat_grad, lat_hat, lat_scale, sg[0], s[0], s[1], slow_count)

    lat_after = from_after(d_lat.reshape(micro, frames, ROWS, CL)[:, 0])
    lat_next = ahead(d_lat, lat_after, next_link)
    lane = lax.broadcasted_iota(jnp.int32, (1, 1, 128), 2)
    rim = jnp.where(lane >= 96, shifted(d_fone, before[..., CM:], link), 0) + jnp.where(
        lane < 32, ahead(d_fone, after[..., CM:], next_link), 0
    )
    ins = w_first.reshape(7, CF, CL + 128)
    own = ins[2:6].reshape(4 * CF, CL + 128)
    lat_prev = jnp.concatenate(
        [jnp.zeros((2 * CF, CL), BF), lateral[: 2 * CF]], 0
    )
    blank = jnp.zeros((CF, 32), BF)
    rim_rows = [
        jnp.concatenate([blank, blank, blank, fast_time[2]], -1),
        jnp.zeros((2 * CF, 128), BF),
        jnp.concatenate([fast_time[0], blank, blank, blank], -1),
    ]
    w_back = jnp.concatenate([own, lat_prev, jnp.concatenate(rim_rows, 0)], -1)
    firsts = jnp.concatenate([d_lat, d_fone, lat_next, rim], -1)
    quad_grad = fast_grad + dot_t(firsts, w_back)
    fast_in_grad = from_quads(quad_grad.astype(BF), micro)
    first_grad = outer(z, jnp.concatenate([d_lat, d_fone], -1))

    def shares(value):
        return value.reshape(devices, -1, value.shape[-1])

    def sent(value):
        return scatter_sum(shares(value)).reshape(-1)

    lateral_grad = first_grad[: 5 * CF, :CL]
    bands = first_grad[:, CL:].reshape(7, CF, 4, CFM)
    ftime_grad = jnp.stack(
        [sum(bands[q + 1 + k, :, q] for q in range(4)) for k in range(3)], 0
    )
    fs = fspace_grad.reshape(3, 4, CFM, 3, 4, CFM)
    fs = sum(fs[:, q, :, :, q] for q in range(4)).transpose(2, 0, 1, 3)
    fo = fout_grad.reshape(4, CFM, 4, CF)
    fo = sum(fo[q, :, q] for q in range(4))
    space_grad = space_grad.reshape(3, CM, 3, CM).transpose(2, 0, 1, 3).reshape(-1, CM)
    time_grad = time_grad.reshape(CS + CL, 3, CM).transpose(1, 0, 2).reshape(-1, CM)
    proj_out = sent(proj_grad)
    out_out = sent(out_grad)
    space_out = sent(space_grad)
    time_out = sent(time_grad)
    flat = [
        part.reshape(devices, -1) for part in (lateral_grad, ftime_grad, fs, fo)
    ]
    sizes = [part.shape[1] for part in flat]
    flat = jnp.concatenate(flat, 1)
    flat = jnp.pad(flat, ((0, 0), (0, -flat.shape[1] % 1024)))
    flat = scatter_sum(flat.reshape(devices, -1, 128)).reshape(-1)
    smalls = []
    at = 0
    for size in sizes:
        smalls.append(flat[at : at + size])
        at += size

    def both(value):
        return jnp.sum(value, 0)

    gain_grad = jnp.concatenate(
        [both(v) for v in (sum_d[1], sum_c[1], sum_b[1], sum_a[1], sum_a[2])]
    )
    bias_grad = jnp.concatenate(
        [both(v) for v in (sum_d[0], sum_c[0], sum_b[0], sum_a[0], sum_a[0])]
    )
    share = slow_gain.shape[0]
    start = lax.axis_index(AXES) * share
    fast_gain_grad = jnp.concatenate(
        [both(fold(sum_c[3]))[:CFM], both(fold(sum_b[3]))[:CFM], both(fold(sum_a[4]))[:CF]]
    )
    fast_bias_grad = jnp.concatenate(
        [both(fold(sum_c[2]))[:CFM], both(fold(sum_b[2]))[:CFM], both(fold(sum_a[3]))[:CF]]
    )
    return (
        slow_out,
        fast_out,
        slow_in_grad,
        fast_in_grad,
        smalls[0],
        time_out,
        space_out,
        out_out,
        proj_out,
        smalls[1],
        smalls[2],
        smalls[3],
        lax.dynamic_slice_in_dim(gain_grad, start, share),
        lax.dynamic_slice_in_dim(bias_grad, start, share),
        fast_gain_grad,
        fast_bias_grad,
    )


def solution(mesh):
    frames = P(None, AXES, None, None)
    flat = P(AXES)
    return jax.shard_map(
        local,
        mesh=mesh,
        in_specs=(frames, frames, P(None, AXES))
        + (flat,) * 10
        + (P(), P(), frames, frames),
        out_specs=(frames,) * 4 + (flat,) * 10 + (P(), P()),
        check_vma=False,
    )
```

time: 1660 us -> 796 us (0.48)
  blocking collectives: 598 us -> 79.8 us
  waiting for transfers between devices: 341 us -> 140 us
  matrix products: 237 us -> 86.2 us
  local copies, waits for them, and re-layouts: 320 us -> 177 us
  other arithmetic: 84.5 us -> 175 us
  starting transfers between devices: 49.5 us -> 108 us
    psum x7 -> x0, blocking collectives: 286 us -> none  [the longest x4 164 us: norm_totals(): joined = lax.psum(jnp.concatenate(firsts + seconds), ('path', 'dp'))]
    unnamed x6 -> x3, waiting for transfers between devices: 225 us -> 0.05 us
    all_gather x4 -> x1, blocking collectives: 268 us -> 79.8 us  [gathered(): return lax.all_gather(shard.reshape(-1, lanes), AXES, axis=0, tiled=True)]
    dot_general x196 -> x21, matrix products: 237 us -> 86.2 us  [the longest x7 32.4 us: dot(): lax.dot_general(left, right, (((left.ndim - 1,), (0,)), ((), ())), prefer...]
    ppermute x16 -> x114, waiting for transfers between devices: 0.04 us -> 139 us  [the longest x106 126 us: swap(): return lax.ppermute(value, AXES, [(i, i ^ bit) for i in range(count)])]
    psum x1 -> x0, waiting for transfers between devices: 116 us -> none  [grad_totals(): joined = lax.psum(jnp.concatenate(vectors), ('path', 'dp'))]
    slice x102 -> x55, local copies, waits for them, and re-layouts: 123 us -> 26.1 us  [the longest x16 7.87 us: roll(): return jnp.where(mask, jnp.roll(value, step, 1), 0)]
    another operation x50 -> x19, local copies, waits for them, and re-layouts: 75.8 us -> 4.1 us  [the longest x4 2.22 us: from_quads(): return jnp.stack(parts, 1).reshape(micro, -1, PIX, lanes)]
  transfers between devices with their start and end apart: 21 -> 117, of which waited for: 2 -> 50; matrix products, arithmetic and copies ran while one was open for 23% -> 41% of each run, Pallas kernels for 0% -> 0%
where the time goes in v1:
time: 796 us; the launch traced here: 784 us
  local copies, waits for them, and re-layouts  177 us (22%)
  other arithmetic  175 us (22%)
  waiting for transfers between devices  140 us (18%)
  starting transfers between devices  108 us (14%)
  matrix products  86.2 us (11%)
  blocking collectives  79.8 us (10%)
  between operations  18.6 us (2%)
    ppermute x106, waiting for transfers between devices, swap(): return lax.ppermute(value, AXES, [(i, i ^ bit) for i in range(count)])  126 us
    ppermute x106, starting transfers between devices, swap(): return lax.ppermute(value, AXES, [(i, i ^ bit) for i in range(count)])  91 us
    all_gather x1, blocking collectives, gathered(): return lax.all_gather(shard.reshape(-1, lanes), AXES, axis=0, tiled=True)  79.8 us
    reduce_sum x41, other arithmetic, sums_of(): jnp.sum(value.reshape((micro, -1) + value.shape[-1:]), 1)  49.9 us
    unnamed x468, local copies, waits for them, and re-layouts  48.3 us
    dot_general x7, matrix products, dot(): lax.dot_general(left, right, (((left.ndim - 1,), (0,)), ((), ())), prefer...  32.4 us
    dot_general x7, matrix products, dot_t(): lax.dot_general(left, right, (((left.ndim - 1,), (1,)), ((), ())), prefer...  27.2 us
    dot_general x7, matrix products, outer(): lax.dot_general(left.reshape(-1, left.shape[-1]), right.reshape(-1, right...  26.6 us
  transfers between devices with their start and end apart: 117, of which 50 were waited for; matrix products, arithmetic and copies ran while one was open for 41% of the time, Pallas kernels for 0%

profile of v1, /device:TPU:0, one launch (start us, length us, event | category | flops | bytes accessed | tf_op | source)
XLA Modules:
  0.0 783.8 jit_solution(4029338011006932963)
XLA Ops:
  10.6 4.2 concatenate.283
  31.3 79.8 %all_gather.15 = bf16[256,1024]{1,0:T(8,128)(2,1)} all-gather(bf16[8,1024]{1,0:T(8,128)(2,1)S(1)} %reshape.1296), channel_id=1, replica_groups=mesh['path'=2,'dp'=16] {'path','dp'}, dimensions={0}, use_global_device_ids=true | all-gather | bytes 540672 | tf_op jit(solution)/shard_map/all_gather | solution.py:266
  111.0 6.8 pad_convert_fusion
  129.3 9.8 %copy.234 = f32[2,4,208,1024]{3,2,1,0:T(8,128)} copy(f32[2,4,208,1024]{3,1,2,0:T(4,128)} %pad_convert_fusion) | data formatting | bytes 13631488 | tf_op jit(solution)/shard_map/convert_element_type | solution.py:414
  139.1 6.0 copy.276
  150.9 7.0 collective-permute-done.6
  211.9 4.6 pad_maximum_fusion.1
  219.0 4.7 fusion.282
  240.2 11.3 %multiply_reduce_fusion.3 = (f32[8,1024]{1,0:T(8,128)}, f32[8,1024]{1,0:T(8,128)}, f32[8,208,1024]{2,1,0:T(8,128)}) fusion(bf16[1280,1024]{1,0:T(8,128)(2,1)} %all-gather.6.cloned.1.call-done, bf16[8,208,256]{2,1,0:T(8,128)(2,1)} %select_convert_fusion.8, bf16[8,208,1024]{2,1,0:T(8,128)(2,1)} %bitcast.759), kind=kOutput, calls=%fused_computation.19 | convolution fusion | flops 4375691264 | bytes 13762560 | tf_op jit(solution)/shard_map/dot_general | solution.py:124
  311.2 4.3 fusion.237
  336.7 4.5 copy.289
  342.7 6.8 fusion.232
  357.8 8.2 %multiply_reduce_fusion.4 = (f32[8,512]{1,0:T(8,128)}, f32[8,512]{1,0:T(8,128)}, f32[8,208,512]{2,1,0:T(8,128)}, bf16[8,208,512]{2,1,0:T(8,128)(2,1)S(1)}) fusion(f32[8,208,512]{2,1,0:T(8,128)} %get-tuple-element.270, f32[8,512]{1,0:T(8,128)S(1)} %mul.1056, f32[8,512]{1,0:T(8,128)S(1)} %sub.241, bf16[8,208,128]{2,1,0:T(8,128)(2,1)} %get-tuple-element.160, ...), kind=kLoop, calls=%fused_computation.42 | loop fusion | flops 36626432 | bytes 11997184 | tf_op jit(solution)/shard_map/reduce_sum | solution.py:216
  382.3 14.4 %multiply_reduce_fusion = (f32[8,1024]{1,0:T(8,128)S(1)}, f32[8,1024]{1,0:T(8,128)S(1)}, f32[8,1024]{1,0:T(8,128)S(1)}, f32[8,208,1024]{2,1,0:T(8,128)}, f32[8,208,1024]{2,1,0:T(8,128)}) fusion(f32[8,208,1024]{2,1,0:T(8,128)} %get-tuple-element.269, f32[8,1024]{1,0:T(8,128)S(1)} %mul.1044, f32[8,1024]{1,0:T(8,128)S(1)} %sub.237, f32[8,1024]{1,0:T(8,128)S(1)} %mul.1038, ...), kind=kLoop, calls=%fused_computation.13 | loop fusion | flops 52797440 | bytes 34324480 | tf_op jit(solution)/shard_map/reduce_sum | solution.py:216
  414.1 6.1 copy.320
  421.7 9.5 %select_convert_fusion.1 = (bf16[8,208,1024]{2,1,0:T(8,128)(2,1)S(1)}, bf16[8,208,1024]{2,1,0:T(8,128)(2,1)S(1)}) fusion(f32[8,208,1024]{2,1,0:T(8,128)} %get-tuple-element.114, f32[8,208,1024]{2,1,0:T(8,128)} %get-tuple-element.271, f32[8,1024]{1,0:T(8,128)S(1)} %div.173, f32[8,1024]{1,0:T(8,128)S(1)} %div.171, f32[8,1024]{1,0:T(8,128)S(1)} %broadcast_multiply_fusion.4, ...), kind=kLoop, calls=%fused_computation.12 | loop fusion | flops 25559040 | bytes 27558096 | tf_op jit(solution)/shard_map/convert_element_type | solution.py:328
  431.2 5.1 fusion.285
  447.1 4.2 select_convert_fusion.2
  462.2 10.1 %fusion.24 = f32[8,208,1280]{2,1,0:T(8,128)} fusion(bf16[8,208,1024]{2,1,0:T(8,128)(2,1)} %copy-done.32, bf16[1280,1024]{1,0:T(8,128)(2,1)S(1)} %copy-done.205), kind=kOutput, calls=%fused_computation.51 | convolution fusion | flops 4362076160 | bytes 14548992 | tf_op jit(solution)/shard_map/dot_general | solution.py:130
  509.6 5.3 fusion.235
  517.6 4.4 copy.290
  522.0 4.8 convolution_bitcast_fusion
  560.5 4.6 collective-permute-start.60
  569.8 5.6 collective-permute-done.60
  578.0 4.6 copy.278
  582.6 7.0 fusion.11
  593.8 7.2 convolution_add_fusion
  626.5 4.2 copy.322
  659.3 4.8 collective-permute-done.102
  737.7 4.7 collective-permute-done.107
  752.8 5.4 collective-permute-done.82
  767.6 4.3 collective-permute-done.112
  (1239 shorter events, 491.1 us)
Async XLA Ops:
  7.2 209.2 %all-gather.4.cloned.1.call-start = ((), (), s32[]{:S(2)}) async-start(), calls=%async_computation | async-start | bytes 2027520 | tf_op jit(solution)/shard_map/all_gather | solution.py:266
  8.9 231.3 %all-gather.6.cloned.1.call-start = ((), (), s32[]{:S(2)}) async-start(), calls=%async_computation.1 | async-start | bytes 2703360 | tf_op jit(solution)/shard_map/all_gather | solution.py:266
  10.5 267.6 %all-gather.8.cloned.1.call-start = ((), (), s32[]{:S(2)}) async-start(), calls=%async_computation.2 | async-start | bytes 1216512 | tf_op jit(solution)/shard_map/all_gather | solution.py:266
  14.8 106.2 %collective-permute-start.3 = (bf16[1,6144]{1,0:T(2,128)(2,1)S(1)}, bf16[1,6144]{1,0:T(2,128)(2,1)S(1)}, u32[]{:S(2)}, u32[]{:S(2)}) collective-permute-start(bf16[1,6144]{1,0:T(2,128)(2,1)S(1)} %broadcast_in_dim.384), channel_id=1, source_target_pairs={{0,1},{1,0},{2,3},{3,2},{4,5},{5,4},{6,7},{7,6},{8,9},{9,8},{10,11... | collective-permute-start | bytes 36872 | tf_op jit(solution)/shard_map/ppermute | solution.py:23
  19.8 138.3 %collective-permute-start = (bf16[2,2,196,128]{3,2,0,1:T(8,128)(2,1)}, bf16[2,2,196,128]{3,2,0,1:T(8,128)(2,1)}, u32[]{:S(2)}, u32[]{:S(2)}) collective-permute-start(bf16[2,2,196,128]{3,2,0,1:T(8,128)(2,1)} %copy.329), channel_id=1, source_target_pairs={{0,1},{1,2},{2,3},{3,4},{4,5},{5,6},{6,7},{7,8},{8,9},{9,10},{10,1... | collective-permute-start | bytes 602120 | tf_op jit(solution)/shard_map/ppermute | solution.py:100
  23.8 126.1 %collective-permute-start.1 = (bf16[2,1,196,128]{3,2,0,1:T(8,128)(2,1)S(1)}, bf16[2,1,196,128]{3,2,0,1:T(8,128)(2,1)}, u32[]{:S(2)}, u32[]{:S(2)}) collective-permute-start(bf16[2,1,196,128]{3,2,0,1:T(8,128)(2,1)S(1)} %copy.334), channel_id=1, source_target_pairs={{1,0},{2,1},{3,2},{4,3},{5,4},{6,5},{7,6},{8,7},{9,8},{10,9},{11,1... | collective-permute-start | bytes 301064 | tf_op jit(solution)/shard_map/ppermute | solution.py:105
  25.2 120.2 %collective-permute-start.2 = (f32[2,1]{1,0:T(2,128)S(1)}, f32[2,1]{1,0:T(2,128)S(1)}, u32[]{:S(2)}, u32[]{:S(2)}) collective-permute-start(f32[2,1]{1,0:T(2,128)S(1)} %bitcast.854), channel_id=1, source_target_pairs={{1,0},{2,1},{3,2},{4,3},{5,4},{6,5},{7,6},{8,7},{9,8},{10,9},{11,1... | collective-permute-start | bytes 32 | tf_op jit(solution)/shard_map/ppermute | solution.py:105
  121.0 24.1 %collective-permute-start.4 = (bf16[2,6144]{1,0:T(2,128)(2,1)S(1)}, bf16[2,6144]{1,0:T(2,128)(2,1)S(1)}, u32[]{:S(2)}, u32[]{:S(2)}) collective-permute-start(bf16[2,6144]{1,0:T(2,128)(2,1)S(1)} %broadcast_select_fusion), channel_id=1, source_target_pairs={{0,2},{1,3},{2,0},{3,1},{4,6},{5,7},{6,4},{7,5},{8,10},{9,11},{10,... | collective-permute-start | bytes 73736 | tf_op jit(solution)/shard_map/ppermute | solution.py:23
  327.2 14.0 %collective-permute-start.28 = (f32[2,1536]{1,0:T(2,128)}, f32[2,1536]{1,0:T(2,128)}, u32[]{:S(2)}, u32[]{:S(2)}) collective-permute-start(f32[2,1536]{1,0:T(2,128)} %add_add_fusion.8), channel_id=1, source_target_pairs={{0,4},{1,5},{2,6},{3,7},{4,0},{5,1},{6,2},{7,3},{8,12},{9,13},{10,... | collective-permute-start | bytes 36872 | tf_op jit(solution)/shard_map/ppermute | solution.py:23
  327.2 14.0 %collective-permute-start.29 = (f32[2,1536]{1,0:T(2,128)}, f32[2,1536]{1,0:T(2,128)}, u32[]{:S(2)}, u32[]{:S(2)}) collective-permute-start(f32[2,1536]{1,0:T(2,128)} %add_add_fusion.8), channel_id=1, source_target_pairs={{0,8},{1,9},{2,10},{3,11},{4,12},{5,13},{6,14},{7,15},{8,0},{9,1},... | collective-permute-start | bytes 36872 | tf_op jit(solution)/shard_map/ppermute | solution.py:23
  328.5 12.7 %collective-permute-start.30 = (f32[2,1536]{1,0:T(2,128)}, f32[2,1536]{1,0:T(2,128)}, u32[]{:S(2)}, u32[]{:S(2)}) collective-permute-start(f32[2,1536]{1,0:T(2,128)} %add_add_fusion.8), channel_id=1, source_target_pairs={{0,12},{1,13},{2,14},{3,15},{4,8},{5,9},{6,10},{7,11},{8,4},{9,5},... | collective-permute-start | bytes 36872 | tf_op jit(solution)/shard_map/ppermute | solution.py:23
  353.6 13.6 %collective-permute-start.31 = (f32[2,2048]{1,0:T(2,128)}, f32[2,2048]{1,0:T(2,128)}, u32[]{:S(2)}, u32[]{:S(2)}) collective-permute-start(f32[2,2048]{1,0:T(2,128)} %pad_maximum_fusion.25), channel_id=1, source_target_pairs={{0,16},{1,17},{2,18},{3,19},{4,20},{5,21},{6,22},{7,23},{8,24},{9,... | collective-permute-start | bytes 49160 | tf_op jit(solution)/shard_map/ppermute | solution.py:23
  453.2 20.0 %collective-permute-start.45 = (f32[2,768]{1,0:T(2,128)S(1)}, f32[2,768]{1,0:T(2,128)S(1)}, u32[]{:S(2)}, u32[]{:S(2)}) collective-permute-start(f32[2,768]{1,0:T(2,128)S(1)} %pad_maximum_fusion.28), channel_id=1, source_target_pairs={{0,16},{1,17},{2,18},{3,19},{4,20},{5,21},{6,22},{7,23},{8,24},{9,... | collective-permute-start | bytes 18440 | tf_op jit(solution)/shard_map/ppermute | solution.py:23
  461.0 222.0 %collective-permute-start.104 = (bf16[2,2,2,2,16,1024]{5,4,1,0,2,3:T(8,128)(2,1)}, bf16[2,2,2,2,16,1024]{5,4,1,0,2,3:T(8,128)(2,1)}, u32[]{:S(2)}, u32[]{:S(2)}) collective-permute-start(bf16[2,2,2,2,16,1024]{5,4,1,0,2,3:T(8,128)(2,1)} %fusion.122), channel_id=1, source_target_pairs={{0,16},{1,17},{2,18},{3,19},{4,20},{5,21},{6,22},{7,23},{8,24},{9,... | collective-permute-start | bytes 1572872 | tf_op jit(solution)/shard_map/ppermute | solution.py:23
  461.5 269.6 %collective-permute-start.109 = (bf16[2,2,2,2,24,1024]{5,4,3,2,1,0:T(8,128)(2,1)}, bf16[2,2,2,2,24,1024]{5,4,3,2,1,0:T(8,128)(2,1)}, u32[]{:S(2)}, u32[]{:S(2)}) collective-permute-start(bf16[2,2,2,2,24,1024]{5,4,3,2,1,0:T(8,128)(2,1)} %fusion.105), channel_id=1, source_target_pairs={{0,16},{1,17},{2,18},{3,19},{4,20},{5,21},{6,22},{7,23},{8,24},{9,... | collective-permute-start | bytes 2359304 | tf_op jit(solution)/shard_map/ppermute | solution.py:23
  515.0 17.9 %collective-permute-start.52 = (f32[2,768]{1,0:T(2,128)S(1)}, f32[2,768]{1,0:T(2,128)S(1)}, u32[]{:S(2)}, u32[]{:S(2)}) collective-permute-start(f32[2,768]{1,0:T(2,128)S(1)} %pad_maximum_fusion.29), channel_id=1, source_target_pairs={{0,16},{1,17},{2,18},{3,19},{4,20},{5,21},{6,22},{7,23},{8,24},{9,... | collective-permute-start | bytes 18440 | tf_op jit(solution)/shard_map/ppermute | solution.py:23
  548.6 11.9 %collective-permute-start.89 = (bf16[2,2,2,2,32,256]{5,4,1,0,2,3:T(8,128)(2,1)}, bf16[2,2,2,2,32,256]{5,4,1,0,2,3:T(8,128)(2,1)}, u32[]{:S(2)}, u32[]{:S(2)}) collective-permute-start(bf16[2,2,2,2,32,256]{5,4,1,0,2,3:T(8,128)(2,1)} %fusion.140), channel_id=1, source_target_pairs={{0,16},{1,17},{2,18},{3,19},{4,20},{5,21},{6,22},{7,23},{8,24},{9,... | collective-permute-start | bytes 786440 | tf_op jit(solution)/shard_map/ppermute | solution.py:23
  549.6 17.4 %collective-permute-start.94 = (bf16[2,2,2,2,40,256]{5,4,3,2,1,0:T(8,128)(2,1)}, bf16[2,2,2,2,40,256]{5,4,3,2,1,0:T(8,128)(2,1)}, u32[]{:S(2)}, u32[]{:S(2)}) collective-permute-start(bf16[2,2,2,2,40,256]{5,4,3,2,1,0:T(8,128)(2,1)} %fusion.136), channel_id=1, source_target_pairs={{0,16},{1,17},{2,18},{3,19},{4,20},{5,21},{6,22},{7,23},{8,24},{9,... | collective-permute-start | bytes 983048 | tf_op jit(solution)/shard_map/ppermute | solution.py:23
  557.1 12.4 %collective-permute-start.59 = (bf16[2,208,384]{2,1,0:T(8,128)(2,1)S(1)}, bf16[2,208,384]{2,1,0:T(8,128)(2,1)S(1)}, u32[]{:S(2)}, u32[]{:S(2)}) collective-permute-start(bf16[2,208,384]{2,1,0:T(8,128)(2,1)S(1)} %get-tuple-element.172), channel_id=1, source_target_pairs={{1,0},{2,1},{3,2},{4,3},{5,4},{6,5},{7,6},{8,7},{9,8},{10,9},{11,1... | collective-permute-start | bytes 958472 | tf_op jit(solution)/shard_map/ppermute | solution.py:105
  560.5 14.9 %collective-permute-start.60 = (bf16[2,208,384]{2,1,0:T(8,128)(2,1)S(1)}, bf16[2,208,384]{2,1,0:T(8,128)(2,1)S(1)}, u32[]{:S(2)}, u32[]{:S(2)}) collective-permute-start(bf16[2,208,384]{2,1,0:T(8,128)(2,1)S(1)} %get-tuple-element.173), channel_id=1, source_target_pairs={{0,1},{1,2},{2,3},{3,4},{4,5},{5,6},{6,7},{7,8},{8,9},{9,10},{10,1... | collective-permute-start | bytes 958472 | tf_op jit(solution)/shard_map/ppermute | solution.py:100
  618.5 12.2 %collective-permute-start.65 = (f32[2,512]{1,0:T(2,128)S(1)}, f32[2,512]{1,0:T(2,128)S(1)}, u32[]{:S(2)}, u32[]{:S(2)}) collective-permute-start(f32[2,512]{1,0:T(2,128)S(1)} %add_add_fusion.16), channel_id=1, source_target_pairs={{0,4},{1,5},{2,6},{3,7},{4,0},{5,1},{6,2},{7,3},{8,12},{9,13},{10,... | collective-permute-start | bytes 12296 | tf_op jit(solution)/shard_map/ppermute | solution.py:23
  618.6 13.6 %collective-permute-start.66 = (f32[2,512]{1,0:T(2,128)S(1)}, f32[2,512]{1,0:T(2,128)S(1)}, u32[]{:S(2)}, u32[]{:S(2)}) collective-permute-start(f32[2,512]{1,0:T(2,128)S(1)} %add_add_fusion.16), channel_id=1, source_target_pairs={{0,8},{1,9},{2,10},{3,11},{4,12},{5,13},{6,14},{7,15},{8,0},{9,1},... | collective-permute-start | bytes 12296 | tf_op jit(solution)/shard_map/ppermute | solution.py:23
  620.9 11.9 %collective-permute-start.67 = (f32[2,512]{1,0:T(2,128)S(1)}, f32[2,512]{1,0:T(2,128)S(1)}, u32[]{:S(2)}, u32[]{:S(2)}) collective-permute-start(f32[2,512]{1,0:T(2,128)S(1)} %add_add_fusion.16), channel_id=1, source_target_pairs={{0,12},{1,13},{2,14},{3,15},{4,8},{5,9},{6,10},{7,11},{8,4},{9,5},... | collective-permute-start | bytes 12296 | tf_op jit(solution)/shard_map/ppermute | solution.py:23
  630.7 16.0 %collective-permute-start.100 = (bf16[2,2,2,8,1024]{4,3,2,1,0:T(8,128)(2,1)}, bf16[2,2,2,8,1024]{4,3,2,1,0:T(8,128)(2,1)}, u32[]{:S(2)}, u32[]{:S(2)}) collective-permute-start(bf16[2,2,2,8,1024]{4,3,2,1,0:T(8,128)(2,1)} %fusion.155), channel_id=1, source_target_pairs={{0,1},{1,0},{2,3},{3,2},{4,5},{5,4},{6,7},{7,6},{8,9},{9,8},{10,11... | collective-permute-start | bytes 393224 | tf_op jit(solution)/shard_map/ppermute | solution.py:23
  632.1 15.7 %collective-permute-start.90 = (bf16[2,2,2,32,256]{4,3,1,0,2:T(8,128)(2,1)}, bf16[2,2,2,32,256]{4,3,1,0,2:T(8,128)(2,1)}, u32[]{:S(2)}, u32[]{:S(2)}) collective-permute-start(bf16[2,2,2,32,256]{4,3,1,0,2:T(8,128)(2,1)} %fusion.154), channel_id=1, source_target_pairs={{0,1},{1,0},{2,3},{3,2},{4,5},{5,4},{6,7},{7,6},{8,9},{9,8},{10,11... | collective-permute-start | bytes 393224 | tf_op jit(solution)/shard_map/ppermute | solution.py:23
  632.7 35.8 %collective-permute-start.95 = (bf16[2,2,2,40,256]{4,3,2,1,0:T(8,128)(2,1)}, bf16[2,2,2,40,256]{4,3,2,1,0:T(8,128)(2,1)}, u32[]{:S(2)}, u32[]{:S(2)}) collective-permute-start(bf16[2,2,2,40,256]{4,3,2,1,0:T(8,128)(2,1)} %fusion.149), channel_id=1, source_target_pairs={{0,2},{1,3},{2,0},{3,1},{4,6},{5,7},{6,4},{7,5},{8,10},{9,11},{10,... | collective-permute-start | bytes 491528 | tf_op jit(solution)/shard_map/ppermute | solution.py:23
  646.7 87.8 %collective-permute-start.79 = (bf16[2,2,2,2,56,256]{5,4,1,0,2,3:T(8,128)(2,1)S(1)}, bf16[2,2,2,2,56,256]{5,4,1,0,2,3:T(8,128)(2,1)S(1)}, u32[]{:S(2)}, u32[]{:S(2)}) collective-permute-start(bf16[2,2,2,2,56,256]{5,4,1,0,2,3:T(8,128)(2,1)S(1)} %copy-done.72), channel_id=1, source_target_pairs={{0,16},{1,17},{2,18},{3,19},{4,20},{5,21},{6,22},{7,23},{8,24},{9,... | collective-permute-start | bytes 1376264 | tf_op jit(solution)/shard_map/ppermute | solution.py:23
  667.9 69.5 %collective-permute-start.84 = (bf16[2,2,2,2,64,256]{5,4,3,2,1,0:T(8,128)(2,1)S(1)}, bf16[2,2,2,2,64,256]{5,4,3,2,1,0:T(8,128)(2,1)S(1)}, u32[]{:S(2)}, u32[]{:S(2)}) collective-permute-start(bf16[2,2,2,2,64,256]{5,4,3,2,1,0:T(8,128)(2,1)S(1)} %copy-done.71), channel_id=1, source_target_pairs={{0,16},{1,17},{2,18},{3,19},{4,20},{5,21},{6,22},{7,23},{8,24},{9,... | collective-permute-start | bytes 1572872 | tf_op jit(solution)/shard_map/ppermute | solution.py:23
  681.7 35.1 %collective-permute-start.68 = (bf16[2,208,256]{2,1,0:T(8,128)(2,1)S(1)}, bf16[2,208,256]{2,1,0:T(8,128)(2,1)S(1)}, u32[]{:S(2)}, u32[]{:S(2)}) collective-permute-start(bf16[2,208,256]{2,1,0:T(8,128)(2,1)S(1)} %slice_bitcast_fusion.15), channel_id=1, source_target_pairs={{1,0},{2,1},{3,2},{4,3},{5,4},{6,5},{7,6},{8,7},{9,8},{10,9},{11,1... | collective-permute-start | bytes 638984 | tf_op jit(solution)/shard_map/ppermute | solution.py:105
  716.7 13.8 %collective-permute-start.105 = (bf16[2,2,2,16,1024]{4,3,1,0,2:T(8,128)(2,1)S(1)}, bf16[2,2,2,16,1024]{4,3,1,0,2:T(8,128)(2,1)S(1)}, u32[]{:S(2)}, u32[]{:S(2)}) collective-permute-start(bf16[2,2,2,16,1024]{4,3,1,0,2:T(8,128)(2,1)S(1)} %fusion.141), channel_id=1, source_target_pairs={{0,1},{1,0},{2,3},{3,2},{4,5},{5,4},{6,7},{7,6},{8,9},{9,8},{10,11... | collective-permute-start | bytes 786440 | tf_op jit(solution)/shard_map/ppermute | solution.py:23
  732.9 19.0 %collective-permute-start.110 = (bf16[2,2,2,24,1024]{4,3,2,1,0:T(8,128)(2,1)S(1)}, bf16[2,2,2,24,1024]{4,3,2,1,0:T(8,128)(2,1)S(1)}, u32[]{:S(2)}, u32[]{:S(2)}) collective-permute-start(bf16[2,2,2,24,1024]{4,3,2,1,0:T(8,128)(2,1)S(1)} %fusion.132), channel_id=1, source_target_pairs={{0,2},{1,3},{2,0},{3,1},{4,6},{5,7},{6,4},{7,5},{8,10},{9,11},{10,... | collective-permute-start | bytes 1179656 | tf_op jit(solution)/shard_map/ppermute | solution.py:23
  752.2 13.5 %collective-permute-start.111 = (bf16[2,2,24,1024]{3,2,1,0:T(8,128)(2,1)S(1)}, bf16[2,2,24,1024]{3,2,1,0:T(8,128)(2,1)S(1)}, u32[]{:S(2)}, u32[]{:S(2)}) collective-permute-start(bf16[2,2,24,1024]{3,2,1,0:T(8,128)(2,1)S(1)} %fusion.147), channel_id=1, source_target_pairs={{0,1},{1,0},{2,3},{3,2},{4,5},{5,4},{6,7},{7,6},{8,9},{9,8},{10,11... | collective-permute-start | bytes 589832 | tf_op jit(solution)/shard_map/ppermute | solution.py:23
  (299 other events, 2278.5 us)
Sparse Core Ops, SparseCore 0:
  11.5 60.3 all-gather.3
  75.3 57.0 all-gather.5
  135.9 54.2 all-gather.7
